TPU v7x, 512 devices: a whole 4x4x16 slice. The times are simulated.
512 devices in a mesh: pair: 64 (over x, z), virt: 8 (over y, core).
Axes of the slice: x: 4, y: 4, z: 16, core: 2. Of those that a mesh axis runs over, the one named last changes fastest.
Arguments:
- amplitudes: float32 [128, 512, 512], P('pair', 'virt'), may hold values from -6 to 6
- integral_store: float32 [8, 64, 128, 128], P('virt', 'pair'), may hold values from -0.1875 to 0.1875
- domains: int32 [128, 4], P('pair'), may hold values from 0 to 7, as said below
- domain_length: int32 [128], P('pair'), may hold values from 1 to 4
- owner_map: int32 [64], replicated, may hold values from 0 to 63, each once
Outputs:
- ladder: float32 [128, 512, 512], P('pair', 'virt')
Inputs may be any that keep to these rules, and one draw needn't show every extreme that they name: `domains`: each row names 4 different tiles; only the first domain_length entries of a row are live.
All inputs are finite; a program needn't handle non-finite values.
Results may differ from a plain program's by a relative error of at most 0.000098.
Values sent between devices are 32-bit elements; how exact they have to be, the bound alone decides.
No kernel may reach another device: no remote copies, remote signals or barrier semaphores. Data moves between devices by JAX's collectives and lax.ppermute only.
A program may use at most 64 MiB of HBM per device.

v0:
```python
import jax
import jax.numpy as jnp
from jax import lax
from jax.sharding import PartitionSpec as P

TILE = 128
M = 4
NT = 8


def ladder_term(matrix, masked):
    half = jnp.einsum("qrc,cd->qrd", matrix, masked, precision=lax.Precision.HIGHEST)
    return jnp.einsum("qrd,qbd->rb", half, matrix, precision=lax.Precision.HIGHEST)


def on_device(amplitudes, integral_store, domains, domain_length, owner_map):
    order = M * TILE
    full_amps = lax.all_gather(amplitudes, "virt", axis=1, tiled=True)
    whole_store = lax.all_gather(integral_store, "pair", axis=1, tiled=True)
    local_q = integral_store.shape[0]
    pairs = amplitudes.shape[0]
    live = (jnp.arange(M)[None, :] < domain_length[:, None]).astype(jnp.float32)
    position = owner_map[domains[:, :, None] * NT + domains[:, None, :]]
    picked = jnp.take(whole_store, position.reshape(-1), axis=1)
    picked = picked.reshape(local_q, pairs, M, M, TILE, TILE)
    picked = picked * (live[:, :, None] * live[:, None, :])[None, :, :, :, None, None]
    matrices = picked.transpose(1, 0, 2, 4, 3, 5).reshape(pairs, local_q, order, order)
    row_live = jnp.repeat(live, TILE, axis=1)
    masked = full_amps * row_live[:, :, None] * row_live[:, None, :]

    def one_pair(items):
        matrix, amp_block, length = items
        return ladder_term(matrix, amp_block)

    terms = lax.map(one_pair, (matrices, masked, domain_length))
    summed = lax.psum(terms, "virt")
    rows = order // lax.axis_size("virt")
    return lax.dynamic_slice_in_dim(summed, lax.axis_index("virt") * rows, rows, 1)


def solution(mesh):
    placed = (
        P("pair", "virt", None),
        P("virt", "pair", None, None),
        P("pair", None),
        P("pair"),
        P(),
    )
    return jax.shard_map(
        on_device, mesh=mesh, in_specs=placed, out_specs=P("pair", "virt", None), check_vma=False
    )
```

profile of v0, /device:TPU:1, one launch (start us, length us, event | category | flops | bytes accessed | tf_op | source)
XLA Modules:
  0.0 299.8 jit_solution(1592998112843832967)
XLA Ops:
  6.5 0.0 copy-start
  6.5 0.0 all-gather.5.cloned.1.call-start
  6.5 0.7 all-gather.5.cloned.1.call-update
  7.3 0.0 all-gather.3.cloned.1.call-start
  7.3 0.7 all-gather.3.cloned.1.call-update
  8.0 0.0 all-reduce.2.cloned.1.call-start
  8.1 0.7 broadcast_multiply_fusion.1
  8.7 0.8 compare_select_fusion.1
  9.5 0.1 reshape.131
  9.6 0.0 copy-done
  9.6 0.0 copy-start.1
  9.6 0.7 gather_fusion
  10.3 0.1 reshape.130
  10.4 0.0 copy-done.1
  10.4 0.1 compare_convert_fusion
  10.5 0.1 broadcast_bitcast_fusion
  10.6 0.1 broadcast_multiply_fusion
  10.7 37.4 %all-gather.5.cloned.1.call-done = f32[2,512,512]{2,1,0:T(8,128)} async-done(((f32[2,64,512]{2,1,0:T(8,128)}), f32[2,512,512]{2,1,0:T(8,128)}) %all-gather.5.cloned.1.call-update) | async-done | bytes 2097168 | tf_op jit(solution)/shard_map/all_gather | solution.py:18
  48.1 3.2 %multiply_multiply_fusion = f32[2,512,512]{2,1,0:T(8,128)} fusion(f32[2,512,512]{2,1,0:T(8,128)} %all-gather.5.cloned.1.call-done, f32[2,512]{1,0:T(2,128)S(1)} %bitcast.44), kind=kLoop, calls=%fused_computation.13 | loop fusion | flops 1048576 | bytes 4198400 | tf_op jit(solution)/shard_map/mul | solution.py:29
  51.3 138.2 %all-gather.3.cloned.1.call-done = f32[1,64,128,128]{3,2,0,1:T(8,128)} async-done(((f32[1,1,128,128]{3,2,0,1:T(8,128)}), f32[1,64,128,128]{3,2,0,1:T(8,128)}) %all-gather.3.cloned.1.call-update) | async-done | bytes 4194320 | tf_op jit(solution)/shard_map/all_gather | solution.py:19
  189.4 2.9 gather_fusion.1
  192.3 0.3 multiply_bitcast_fusion
  192.6 2.7 copy.9
  195.3 2.1 reshape.128
  197.4 11.9 %while.10 = (s32[]{:T(128)}, f32[2,512,512]{2,1,0:T(8,128)}, f32[2,1,512,512]{3,2,1,0:T(8,128)S(1)}, f32[2,512,512]{2,1,0:T(8,128)}, s32[]{:T(128)}) while((s32[]{:T(128)}, f32[2,512,512]{2,1,0:T(8,128)}, f32[2,1,512,512]{3,2,1,0:T(8,128)S(1)}, f32[2,512,512]{2,1,0:T(8,128)}, s32[]{:T(128)}) %tuple.18), condition=%wide.region_1.2_spmd, body=%wide.region_0.1_spmd.sunk | while | flops 3221225472 | bytes 6293565 | solution.py:35
  197.4 3.1 %fusion.22 = f32[512,512]{1,0:T(8,128)S(1)} fusion(f32[2,512,512]{2,1,0:T(8,128)} %get-tuple-element.74, s32[]{:T(128)} %get-tuple-element.66, f32[2,1,512,512]{3,2,1,0:T(8,128)S(1)} %get-tuple-element.73), kind=kOutput, calls=%fused_computation.4.clone.1 | convolution fusion | flops 1610612736 | bytes 3146752 | tf_op jit(solution)/shard_map/while/body/eval_jaxpr/qrc,cd->qrd/dot_general | solution.py:12
  200.5 2.9 fusion.23
  203.4 3.1 %fusion.22 = f32[512,512]{1,0:T(8,128)S(1)} fusion(f32[2,512,512]{2,1,0:T(8,128)} %get-tuple-element.74, s32[]{:T(128)} %get-tuple-element.66, f32[2,1,512,512]{3,2,1,0:T(8,128)S(1)} %get-tuple-element.73), kind=kOutput, calls=%fused_computation.4.clone.1 | convolution fusion | flops 1610612736 | bytes 3146752 | tf_op jit(solution)/shard_map/while/body/eval_jaxpr/qrc,cd->qrd/dot_general | solution.py:12
  206.4 2.9 fusion.23
  209.3 0.0 all-reduce.2.cloned.1.call-update
  209.3 82.3 %all-reduce.2.cloned.1.call-done = f32[2,512,512]{2,1,0:T(8,128)} async-done(((f32[2,512,512]{2,1,0:T(8,128)}), f32[2,512,512]{2,1,0:T(8,128)}) %all-reduce.2.cloned.1.call-update) | async-done | bytes 2097168 | tf_op jit(solution)/shard_map/psum | solution.py:36
  291.6 1.7 constant_dynamic-slice_fusion
  (6 shorter events, 0.0 us)
Async XLA Ops:
  6.5 3.1 %copy-start = (s32[64]{0:T(128)S(1)}, s32[64]{0:T(128)}, u32[]{:S(2)}) copy-start(s32[64]{0:T(128)} %param.11) | copy-start | bytes 772
  6.5 41.6 %all-gather.5.cloned.1.call-start = ((), (), s32[]{:S(2)}) async-start(), calls=%async_computation.1 | async-start | bytes 2359296 | tf_op jit(solution)/shard_map/all_gather | solution.py:18
  7.3 182.2 %all-gather.3.cloned.1.call-start = ((), (), s32[]{:S(2)}) async-start(), calls=%async_computation | async-start | bytes 4259840 | tf_op jit(solution)/shard_map/all_gather | solution.py:19
  8.0 283.6 %all-reduce.2.cloned.1.call-start = ((), (), s32[]{:S(2)}) async-start(), calls=%async_computation.2 | async-start | bytes 4194304 | tf_op jit(solution)/shard_map/psum | solution.py:36
  9.6 0.8 copy-start.1
Sparse Core Ops, SparseCore 0:
  9.5 38.5 all-gather.4
  51.1 138.3 all-gather.2
  209.5 82.1 all-reduce.1
where the time goes:
time: 301 us; the launch traced here: 300 us
  waiting for transfers between devices  259 us (86%)
  between operations  13.2 us (4%)
  matrix products  11.9 us (4%)
  local copies, waits for them, and re-layouts  10.3 us (3%)
  other arithmetic  5.04 us (2%)
    all_gather x1, waiting for transfers between devices, on_device(): whole_store = lax.all_gather(integral_store, 'pair', axis=1, tiled=True)  138 us
    psum x1, waiting for transfers between devices, on_device(): summed = lax.psum(terms, 'virt')  82.3 us
    all_gather x1, waiting for transfers between devices, on_device(): full_amps = lax.all_gather(amplitudes, 'virt', axis=1, tiled=True)  37.4 us
    dot_general x2, matrix products, ladder_term(): jnp.einsum('qrc,cd->qrd', matrix, masked, precision=lax.Precision.HIGHEST)  6.15 us
  transfers between devices with their start and end apart: 3, of which 3 were waited for; matrix products, arithmetic and copies ran while one was open for 2% of the time, Pallas kernels for 0%

commit v1 on v0

v1 whole, which is shorter than its diff:
```python
import jax
import jax.numpy as jnp
from jax import lax
from jax.experimental import pallas as pl
from jax.experimental.pallas import tpu as pltpu
from jax.sharding import Mesh, PartitionSpec as P

TILE = 128
M = 4
NT = 8
MT = M * TILE
X, ZH, ZL, Y, C = 4, 8, 2, 4, 2
SLICE = TILE // X
KINDS = M * M
f32, bf16 = jnp.float32, jnp.bfloat16
VMEM = pl.BlockSpec(memory_space=pltpu.VMEM)
SMEM = pl.BlockSpec(memory_space=pltpu.SMEM)


def pack_kernel(domains, owner_map, store, out):
    lane = lax.broadcasted_iota(jnp.int32, (8, TILE), 1)
    wanted = jnp.zeros((8, TILE), jnp.int32)
    for p in range(2):
        for a in range(M):
            for c in range(M):
                place = owner_map[domains[p, a] * NT + domains[p, c]]
                wanted = jnp.where(lane == p * KINDS + a * M + c, place, wanted)
    wanted = wanted.astype(f32)
    for x in range(X):
        out[x, :SLICE, :] = store[x * SLICE:(x + 1) * SLICE, :]
        out[x, SLICE:, :] = wanted


def pick_kernel(wanted, parity, own, other, out):
    def body(i, _):
        place = wanted[i]
        at = lax.div(place, ZH * ZL)
        z = lax.rem(place, ZH * ZL)
        row = lax.div(z, ZL) * X + at
        mine = lax.rem(z, ZL) == parity[0]
        out[i] = jnp.where(mine, own[row], other[row])
        return 0

    lax.fori_loop(0, X * C * KINDS, body, 0, unroll=8)


def split(value):
    high = value.astype(bf16)
    return high, (value - high.astype(f32)).astype(bf16)


def product(left, right, dims):
    def one(a, b):
        return lax.dot_general(a, b, (dims, ((), ())), preferred_element_type=f32)

    return one(left[0], right[0]) + (one(left[0], right[1]) + one(left[1], right[0]))


def ladder_kernel(core, lengths, tiles, amps, out, d_high, d_low, t_high, t_low):
    length = lengths[core[0]]
    live = [jnp.where(a < length, 1.0, 0.0).astype(f32) for a in range(M)]
    for q in range(C):
        for a in range(M):
            for c in range(M):
                keep = live[a] * live[c]
                for x in range(X):
                    high, low = split(tiles[x * C + q, a * M + c] * keep)
                    at = a * TILE + x * SLICE
                    d_high[q, at:at + SLICE, c * TILE:(c + 1) * TILE] = high
                    d_low[q, at:at + SLICE, c * TILE:(c + 1) * TILE] = low
    rows = MT // (Y * C)
    for v in range(Y * C):
        for c in range(M):
            high, low = split(amps[v, 0, :, c * TILE:(c + 1) * TILE] * (live[v * rows // TILE] * live[c]))
            t_high[v * rows:(v + 1) * rows, c * TILE:(c + 1) * TILE] = high
            t_low[v * rows:(v + 1) * rows, c * TILE:(c + 1) * TILE] = low
    for r in range(2):
        at = slice(r * 256, (r + 1) * 256)
        total = None
        for q in range(C):
            half = product((d_high[q, at], d_low[q, at]), (t_high[...], t_low[...]), ((1,), (0,)))
            term = product(split(half), (d_high[q], d_low[q]), ((1,), (1,)))
            total = term if total is None else total + term
        out[r * 4:(r + 1) * 4] = total.reshape(4, rows, MT)


def on_device(amplitudes, integral_store, domains, domain_length, owner_map):
    pairs, rows, _ = amplitudes.shape
    core = lax.axis_index("c").astype(jnp.int32).reshape(1)
    parity = lax.axis_index("zl").astype(jnp.int32).reshape(1)
    amps = lax.all_gather(amplitudes, ("y", "c"), axis=0, tiled=False)

    packed = pl.pallas_call(
        pack_kernel,
        out_shape=jax.ShapeDtypeStruct((X, SLICE + 8, TILE), f32),
        in_specs=[SMEM, SMEM, VMEM],
        out_specs=VMEM,
    )(domains, owner_map, integral_store.reshape(TILE, TILE))
    spread = lax.all_to_all(packed, "x", split_axis=0, concat_axis=0, tiled=True)
    wanted = spread[:, SLICE, :pairs * KINDS].astype(jnp.int32).reshape(-1)
    own = lax.all_gather(spread[:, :SLICE], "zh", axis=0, tiled=True)
    other = lax.ppermute(own, "zl", [(0, 1), (1, 0)])

    picked = pl.pallas_call(
        pick_kernel,
        out_shape=jax.ShapeDtypeStruct((X * C * KINDS, SLICE, TILE), f32),
        in_specs=[SMEM, SMEM, VMEM, VMEM],
        out_specs=VMEM,
    )(wanted, parity, own, other)
    tiles = lax.all_to_all(
        picked.reshape(X * C, KINDS, SLICE, TILE), ("x", "c"), split_axis=0, concat_axis=0, tiled=True
    )

    terms = pl.pallas_call(
        ladder_kernel,
        out_shape=jax.ShapeDtypeStruct((Y * C, rows, MT), f32),
        grid_spec=pltpu.PrefetchScalarGridSpec(
            num_scalar_prefetch=2,
            grid=(1,),
            in_specs=[
                pl.BlockSpec((X * C, KINDS, SLICE, TILE), lambda i, core, lengths: (0, 0, 0, 0)),
                pl.BlockSpec((Y * C, 1, rows, MT), lambda i, core, lengths: (0, core[0], 0, 0)),
            ],
            out_specs=pl.BlockSpec((Y * C, rows, MT), lambda i, core, lengths: (0, 0, 0)),
            scratch_shapes=[
                pltpu.VMEM((C, MT, MT), bf16),
                pltpu.VMEM((C, MT, MT), bf16),
                pltpu.VMEM((MT, MT), bf16),
                pltpu.VMEM((MT, MT), bf16),
            ],
        ),
        compiler_params=pltpu.CompilerParams(vmem_limit_bytes=40 * 2**20),
    )(core, domain_length, tiles, amps)
    parts = lax.all_to_all(terms, ("y", "c"), split_axis=0, concat_axis=0, tiled=True)
    return parts.reshape(Y, pairs, rows, MT).sum(0)


def solution(mesh):
    cut = Mesh(mesh.devices.reshape(X, ZH, ZL, Y, C), ("x", "zh", "zl", "y", "c"))
    pair, virt = ("x", "zh", "zl"), ("y", "c")
    placed = (
        P(pair, virt, None),
        P(virt, pair, None, None),
        P(pair, None),
        P(pair),
        P(),
    )
    return jax.shard_map(
        on_device, mesh=cut, in_specs=placed, out_specs=P(pair, virt, None), check_vma=False
    )
```

time: 301 us -> 138 us (0.46)
  waiting for transfers between devices: 259 us -> 33.9 us
  blocking collectives: 0 us -> 61.3 us
  starting transfers between devices: 0.08 us -> 15.1 us
  matrix products: 11.9 us -> 0 us
  Pallas kernels: 0 us -> 9.62 us
  local copies, waits for them, and re-layouts: 10.3 us -> 3.01 us
  other arithmetic: 5.04 us -> 0.81 us
    all_gather x2 -> x1, waiting for transfers between devices: 176 us -> 0.01 us  [on_device(): amps = lax.all_gather(amplitudes, ('y', 'c'), axis=0, tiled=False)]
    psum x1 -> x0, waiting for transfers between devices: 82.3 us -> none  [on_device(): summed = lax.psum(terms, 'virt')]
    all_gather x0 -> x1, blocking collectives: none -> 31.6 us  [on_device(): own = lax.all_gather(spread[:, :SLICE], 'zh', axis=0, tiled=True)]
    all_to_all x0 -> x2, blocking collectives: none -> 29.7 us  [the longest x1 20.3 us: on_device(): lax.all_to_all(terms, ('y', 'c'), split_axis=0, concat_axis=0, tiled=True)]
    all_to_all x0 -> x1, waiting for transfers between devices: none -> 26.4 us  [on_device(): lax.all_to_all(picked.reshape(X * C, KINDS, SLICE, TILE), ('x', 'c'), spl...]
    all_to_all x0 -> x1, starting transfers between devices: none -> 11.9 us  [on_device(): lax.all_to_all(picked.reshape(X * C, KINDS, SLICE, TILE), ('x', 'c'), spl...]
    dot_general x4 -> x0, matrix products: 11.9 us -> none  [the longest x2 6.15 us: ladder_term(): jnp.einsum('qrc,cd->qrd', matrix, masked, precision=lax.Precision.HIGHEST)]
    pallas_call x0 -> x3, Pallas kernels: none -> 9.62 us  [the longest x1 4.55 us: on_device(): pl.pallas_call(ladder_kernel, out_shape=jax.ShapeDtypeStruct((Y * C, rows...]
  transfers between devices with their start and end apart: 3 -> 3, of which waited for: 3 -> 2; matrix products, arithmetic and copies ran while one was open for 2% -> 0% of each run, Pallas kernels for 0% -> 4%
where the time goes in v1:
time: 138 us; the launch traced here: 137 us
  blocking collectives  61.3 us (44%)
  waiting for transfers between devices  33.9 us (25%)
  starting transfers between devices  15.1 us (11%)
  between operations  13.4 us (10%)
  Pallas kernels  9.62 us (7%)
  local copies, waits for them, and re-layouts  3.01 us (2%)
    all_gather x1, blocking collectives, on_device(): own = lax.all_gather(spread[:, :SLICE], 'zh', axis=0, tiled=True)  31.6 us
    all_to_all x1, waiting for transfers between devices, on_device(): lax.all_to_all(picked.reshape(X * C, KINDS, SLICE, TILE), ('x', 'c'), spl...  26.4 us
    all_to_all x1, blocking collectives, on_device(): lax.all_to_all(terms, ('y', 'c'), split_axis=0, concat_axis=0, tiled=True)  20.3 us
    all_to_all x1, starting transfers between devices, on_device(): lax.all_to_all(picked.reshape(X * C, KINDS, SLICE, TILE), ('x', 'c'), spl...  11.9 us
    all_to_all x1, blocking collectives, on_device(): lax.all_to_all(packed, 'x', split_axis=0, concat_axis=0, tiled=True)  9.4 us
    ppermute x1, waiting for transfers between devices, on_device(): other = lax.ppermute(own, 'zl', [(0, 1), (1, 0)])  6.84 us
    pallas_call x1, Pallas kernels, on_device(): pl.pallas_call(ladder_kernel, out_shape=jax.ShapeDtypeStruct((Y * C, rows...  4.55 us
    pallas_call x1, Pallas kernels, on_device(): pl.pallas_call(pick_kernel, out_shape=jax.ShapeDtypeStruct((X * C * KINDS...  3.55 us
  transfers between devices with their start and end apart: 3, of which 2 were waited for; matrix products, arithmetic and copies ran while one was open for 0% of the time, Pallas kernels for 4%

profile of v1, /device:TPU:1, one launch (start us, length us, event | category | flops | bytes accessed | tf_op | source)
XLA Modules:
  0.0 137.2 jit_solution(6799234819948783895)
XLA Ops:
  6.5 0.0 all-gather.3.cloned.1.call-start
  6.5 0.7 all-gather.3.cloned.1.call-update
  7.3 1.5 %shard_map.55 = f32[4,40,128]{2,1,0:T(8,128)} custom-call(s32[2,4]{1,0:T(2,128)} %domains.1, s32[64]{0:T(128)} %owner_map.1, f32[128,128]{1,0:T(8,128)} %bitcast.9), custom_call_target="tpu_custom_call" | custom-call | tf_op jit(solution)/shard_map/pallas_call | solution.py:93
  8.8 9.4 %all_to_all.15 = f32[4,40,128]{2,1,0:T(8,128)S(1)} all-to-all(f32[4,40,128]{2,1,0:T(8,128)} %shard_map.55), channel_id=1, replica_groups=mesh['x'=4,'zh'=8,'zl'=2,'y'=4,'c'=2] {'x'}, dimensions={0} | all-to-all | bytes 163840 | tf_op jit(solution)/shard_map/all_to_all | solution.py:99
  18.2 31.6 %all_gather.9.own = f32[32,32,128]{2,1,0:T(8,128)S(1)} all-gather(f32[4,32,128]{2,1,0:T(8,128)S(1)} %slice.9), channel_id=1, replica_groups=mesh['x'=4,'zh'=8,'zl'=2,'y'=4,'c'=2] {'zh'}, dimensions={0}, use_global_device_ids=true | all-gather | bytes 589824 | tf_op jit(solution)/shard_map/all_gather | solution.py:101
  49.8 0.0 copy-start.2
  49.8 3.1 %collective-permute-start = (f32[32,32,128]{2,1,0:T(8,128)S(1)}, f32[32,32,128]{2,1,0:T(8,128)S(1)}, u32[]{:S(2)}, u32[]{:S(2)}) collective-permute-start(f32[32,32,128]{2,1,0:T(8,128)S(1)} %all_gather.9.own), channel_id=1, source_target_pairs={{0,8},{8,0},{1,9},{9,1},{2,10},{10,2},{3,11},{11,3},{4,12},{12,4},... | collective-permute-start | bytes 1572872 | tf_op jit(solution)/shard_map/ppermute | solution.py:102
  53.0 0.6 convert_element_type.8.wanted
  53.6 6.8 %collective-permute-done.other = f32[32,32,128]{2,1,0:T(8,128)S(1)} collective-permute-done((f32[32,32,128]{2,1,0:T(8,128)S(1)}, f32[32,32,128]{2,1,0:T(8,128)S(1)}, u32[]{:S(2)}, u32[]{:S(2)}) %collective-permute-start) | collective-permute-done | bytes 524320 | tf_op jit(solution)/shard_map/ppermute | solution.py:102
  60.4 0.0 copy-start.3
  60.4 0.0 copy-done.2
  60.4 0.8 copy-done.3
  61.2 3.5 %shard_map.56 = f32[128,32,128]{2,1,0:T(8,128)} custom-call(s32[128]{0:T(128)} %convert_element_type.8.wanted, s32[1]{0:T(128)} %bitcast.2.parity, f32[32,32,128]{2,1,0:T(8,128)} %copy-done.2, f32[32,32,128]{2,1,0:T(8,128)} %copy-done.3), custom_call_target="tpu_custom_call" | custom-call | tf_op jit(solution)/shard_map/pallas_call | solution.py:104
  64.8 0.0 copy-start.1
  64.8 11.9 %all-to-all-start.1 = ((f32[8,16,32,128]{3,2,1,0:T(8,128)}), f32[8,16,32,128]{3,2,1,0:T(8,128)S(1)}, u32[]{:S(2)}, u32[]{:S(2)}) async-start(f32[8,16,32,128]{3,2,1,0:T(8,128)} %bitcast.7), calls=%async_computation.1 | async-start | bytes 4194304 | tf_op jit(solution)/shard_map/all_to_all | solution.py:110
  76.7 26.4 %all-to-all-done.1.tiles = f32[8,16,32,128]{3,2,1,0:T(8,128)S(1)} async-done(((f32[8,16,32,128]{3,2,1,0:T(8,128)}), f32[8,16,32,128]{3,2,1,0:T(8,128)S(1)}, u32[]{:S(2)}, u32[]{:S(2)}) %all-to-all-start.1) | async-done | bytes 2097184 | tf_op jit(solution)/shard_map/all_to_all | solution.py:110
  103.1 0.0 all-gather.3.cloned.1.call-done
  103.1 0.0 copy-done.1
  103.1 0.0 copy-start
  103.1 1.6 %copy-done = f32[16,64,512]{2,1,0:T(8,128)S(1)} copy-done((f32[16,64,512]{2,1,0:T(8,128)S(1)}, f32[16,64,512]{2,1,0:T(8,128)}, u32[]{:S(2)}) %copy-start) | copy-done | bytes 2097176
  104.7 4.6 %shard_map.57 = f32[8,64,512]{2,1,0:T(8,128)S(1)} custom-call(s32[1]{0:T(128)} %bitcast.core, s32[2]{0:T(128)S(1)} %copy-done.1, f32[8,16,32,128]{3,2,1,0:T(8,128)S(1)} %all-to-all-done.1.tiles, f32[8,2,64,512]{3,2,1,0:T(8,128)S(1)} %bitcast.6), custom_call_target="tpu_custom_call" | custom-call | tf_op jit(solution)/shard_map/pallas_call | solution.py:114
  109.2 20.3 %all_to_all.16 = f32[8,64,512]{2,1,0:T(8,128)S(1)} all-to-all(f32[8,64,512]{2,1,0:T(8,128)S(1)} %shard_map.57), channel_id=1, replica_groups=mesh['x'=4,'zh'=8,'zl'=2,'y'=4,'c'=2] {'y','c'}, dimensions={0} | all-to-all | bytes 2097152 | tf_op jit(solution)/shard_map/all_to_all | solution.py:134
  129.5 0.8 reduce_sum.9
  (2 shorter events, 0.0 us)
Async XLA Ops:
  6.5 96.5 %all-gather.3.cloned.1.call-start = ((), (), s32[]{:S(2)}) async-start(), calls=%async_computation.3 | async-start | bytes 2359296 | tf_op jit(solution)/shard_map/all_gather | solution.py:91
  49.8 10.6 %copy-start.2 = (f32[32,32,128]{2,1,0:T(8,128)}, f32[32,32,128]{2,1,0:T(8,128)S(1)}, u32[]{:S(2)}) copy-start(f32[32,32,128]{2,1,0:T(8,128)S(1)} %all_gather.9.own) | copy-start | bytes 1572868
  49.8 10.6 %collective-permute-start = (f32[32,32,128]{2,1,0:T(8,128)S(1)}, f32[32,32,128]{2,1,0:T(8,128)S(1)}, u32[]{:S(2)}, u32[]{:S(2)}) collective-permute-start(f32[32,32,128]{2,1,0:T(8,128)S(1)} %all_gather.9.own), channel_id=1, source_target_pairs={{0,8},{8,0},{1,9},{9,1},{2,10},{10,2},{3,11},{11,3},{4,12},{12,4},... | collective-permute-start | bytes 1572872 | tf_op jit(solution)/shard_map/ppermute | solution.py:102
  60.4 0.8 copy-start.3
  64.8 38.3 %copy-start.1 = (s32[2]{0:T(128)S(1)}, s32[2]{0:T(128)}, u32[]{:S(2)}) copy-start(s32[2]{0:T(128)} %lengths.1) | copy-start | bytes 28
  64.8 38.3 %all-to-all-start.1 = ((f32[8,16,32,128]{3,2,1,0:T(8,128)}), f32[8,16,32,128]{3,2,1,0:T(8,128)S(1)}, u32[]{:S(2)}, u32[]{:S(2)}) async-start(f32[8,16,32,128]{3,2,1,0:T(8,128)} %bitcast.7), calls=%async_computation.1 | async-start | bytes 4194304 | tf_op jit(solution)/shard_map/all_to_all | solution.py:110
  103.1 1.6 %copy-start = (f32[16,64,512]{2,1,0:T(8,128)S(1)}, f32[16,64,512]{2,1,0:T(8,128)}, u32[]{:S(2)}) copy-start(f32[16,64,512]{2,1,0:T(8,128)} %all-gather.3.cloned.1.call-done) | copy-start | bytes 6291460
Sparse Core Ops, SparseCore 0:
  9.5 38.5 all-gather.2

commit v2 on v1

v2 whole, which is shorter than its diff:
```python
import jax
import jax.numpy as jnp
from jax import lax
from jax.experimental import pallas as pl
from jax.experimental.pallas import tpu as pltpu
from jax.sharding import Mesh, PartitionSpec as P

TILE = 128
M = 4
NT = 8
MT = M * TILE
X, ZH, ZL, Y, C = 4, 8, 2, 4, 2
G = X * ZL
SLICE = TILE // G
KINDS = M * M
f32, bf16 = jnp.float32, jnp.bfloat16
VMEM = pl.BlockSpec(memory_space=pltpu.VMEM)
SMALL = pltpu.CompilerParams(vmem_limit_bytes=16 * 2**20)
SMEM = pl.BlockSpec(memory_space=pltpu.SMEM)
ANY = pl.BlockSpec(memory_space=pl.ANY)


def pack_kernel(domains, owner_map, store, out):
    lane = lax.broadcasted_iota(jnp.int32, (8, TILE), 1)
    wanted = jnp.zeros((8, TILE), jnp.int32)
    for p in range(C):
        for a in range(M):
            for c in range(M):
                place = owner_map[domains[p, a] * NT + domains[p, c]]
                wanted = jnp.where(lane == p * KINDS + a * M + c, place, wanted)
    z = lax.rem(wanted, ZH * ZL)
    wanted = lax.div(z, ZL) * G + lax.div(wanted, ZH * ZL) * ZL + lax.rem(z, ZL)
    wanted = wanted.astype(f32)
    for g in range(G):
        out[g, :SLICE, :] = store[g * SLICE:(g + 1) * SLICE, :]
        out[g, SLICE:, :] = wanted


def pick_kernel(wanted, core, own, other, out, held, sems):
    first = core[0] * KINDS
    copies = []
    for g in range(G):
        for k in range(KINDS):
            row = wanted[g * C * KINDS + first + k]
            held[g, 0, k] = own[row]
            held[g, 1, k] = other[row]
        copies.append(pltpu.make_async_copy(held.at[g], out.at[g], sems.at[g]))
        copies[-1].start()
    for copy in copies:
        copy.wait()


def split(value):
    high = value.astype(bf16)
    return high, (value - high.astype(f32)).astype(bf16)


def product(left, right, dims):
    def one(a, b):
        return lax.dot_general(a, b, (dims, ((), ())), preferred_element_type=f32)

    return one(left[0], right[0]) + (one(left[0], right[1]) + one(left[1], right[0]))


def live_tiles(core, lengths):
    length = lengths[core[0]]
    return [jnp.where(a < length, 1.0, 0.0).astype(f32) for a in range(M)]


def mask_kernel(core, tile, lengths, amps, out):
    live = live_tiles(core, lengths)
    keep = jnp.where(tile[0] < lengths[core[0]], 1.0, 0.0).astype(f32)
    for c in range(M):
        at = slice(c * TILE, (c + 1) * TILE)
        high, low = split(amps[:, at] * (keep * live[c]))
        out[0, :, at] = high
        out[1, :, at] = low


def ladder_kernel(core, places, lengths, tiles, m0, m1, m2, m3, out, d_high, d_low, amps, sems):
    fetches = []
    for i, part in enumerate((m0, m1, m2, m3)):
        rows = pl.ds(pl.multiple_of(places[i] * TILE, TILE), TILE)
        fetches.append(pltpu.make_async_copy(part, amps.at[:, rows], sems.at[i]))
        fetches[-1].start()
    live = live_tiles(core, lengths)
    for q in range(C):
        for a in range(M):
            for c in range(M):
                keep = live[a] * live[c]
                for g in range(G):
                    at = a * TILE + g * SLICE
                    at = (q, slice(at, at + SLICE), slice(c * TILE, (c + 1) * TILE))
                    d_high[at], d_low[at] = split(tiles[g, q, a * M + c] * keep)
    for fetch in fetches:
        fetch.wait()
    rows = MT // (Y * C)
    for r in range(2):
        at = slice(r * 256, (r + 1) * 256)
        total = None
        for q in range(C):
            half = product((d_high[q, at], d_low[q, at]), (amps[0], amps[1]), ((1,), (0,)))
            term = product(split(half), (d_high[q], d_low[q]), ((1,), (1,)))
            total = term if total is None else total + term
        out[r * 4:(r + 1) * 4] = total.reshape(4, rows, MT)


def on_device(amplitudes, integral_store, domains, domain_length, owner_map):
    pairs, rows, _ = amplitudes.shape
    core = lax.axis_index("c").astype(jnp.int32).reshape(1)
    plane = lax.axis_index("y").astype(jnp.int32).reshape(1)

    packed = pl.pallas_call(
        pack_kernel,
        out_shape=jax.ShapeDtypeStruct((G, SLICE + 8, TILE), f32),
        in_specs=[SMEM, SMEM, VMEM],
        out_specs=VMEM,
    )(domains, owner_map, integral_store.reshape(TILE, TILE))
    spread = lax.all_to_all(packed, ("x", "zl"), split_axis=0, concat_axis=0, tiled=True)
    wanted = spread[:, SLICE, :pairs * KINDS].astype(jnp.int32).reshape(-1)
    own = lax.all_gather(spread[:, :SLICE], "zh", axis=0, tiled=True)
    other = lax.ppermute(own, "c", [(0, 1), (1, 0)])
    picked = pl.pallas_call(
        pick_kernel,
        out_shape=jax.ShapeDtypeStruct((G, C, KINDS, SLICE, TILE), f32),
        in_specs=[SMEM, SMEM, VMEM, VMEM],
        out_specs=ANY,
        scratch_shapes=[pltpu.VMEM((G, C, KINDS, SLICE, TILE), f32), pltpu.SemaphoreType.DMA((G,))],
        compiler_params=SMALL,
    )(wanted, core, own, other)
    picked, amplitudes = lax.optimization_barrier((picked, amplitudes))
    tiles = lax.all_to_all(picked, ("x", "zl"), split_axis=0, concat_axis=0, tiled=True)

    mine = lax.axis_index("c")
    given = lax.dynamic_index_in_dim(amplitudes, 1 - mine, 0, keepdims=False)
    got = lax.ppermute(given, "c", [(0, 1), (1, 0)])
    kept = lax.dynamic_index_in_dim(amplitudes, mine, 0, keepdims=False)
    block = jnp.where(mine == 0, jnp.concatenate([kept, got]), jnp.concatenate([got, kept]))
    before, across, after = (
        lax.ppermute(block, "y", [(y, (y + step) % Y) for y in range(Y)]) for step in (1, 2, 3)
    )
    places = [lax.rem(plane + Y - step, Y) for step in range(Y)]
    masked = [
        pl.pallas_call(
            mask_kernel,
            out_shape=jax.ShapeDtypeStruct((2, TILE, MT), bf16),
            in_specs=[SMEM, SMEM, SMEM, VMEM],
            out_specs=VMEM,
            compiler_params=SMALL,
        )(core, place, domain_length, part)
        for place, part in zip(places, (block, before, across, after))
    ]
    terms = pl.pallas_call(
        ladder_kernel,
        out_shape=jax.ShapeDtypeStruct((Y * C, rows, MT), f32),
        in_specs=[SMEM, SMEM, SMEM, VMEM, ANY, ANY, ANY, ANY],
        out_specs=VMEM,
        scratch_shapes=[
            pltpu.VMEM((C, MT, MT), bf16),
            pltpu.VMEM((C, MT, MT), bf16),
            pltpu.VMEM((2, MT, MT), bf16),
            pltpu.SemaphoreType.DMA((Y,)),
        ],
        compiler_params=pltpu.CompilerParams(vmem_limit_bytes=24 * 2**20),
    )(core, jnp.concatenate(places), domain_length, tiles, *masked)
    parts = lax.all_to_all(terms, ("y", "c"), split_axis=0, concat_axis=0, tiled=True)
    return parts.reshape(Y, pairs, rows, MT).sum(0)


def solution(mesh):
    cut = Mesh(mesh.devices.reshape(X, ZH, ZL, Y, C), ("x", "zh", "zl", "y", "c"))
    pair, virt = ("x", "zh", "zl"), ("y", "c")
    placed = (
        P(pair, virt, None),
        P(virt, pair, None, None),
        P(pair, None),
        P(pair),
        P(),
    )
    return jax.shard_map(
        on_device, mesh=cut, in_specs=placed, out_specs=P(pair, virt, None), check_vma=False
    )
```

time: 138 us -> 115 us (0.83)
  waiting for transfers between devices: 33.9 us -> 9.12 us
  between operations: 13.4 us -> 0.19 us
  starting transfers between devices: 15.1 us -> 25.9 us
  blocking collectives: 61.3 us -> 63.7 us
  local copies, waits for them, and re-layouts: 3.01 us -> 4.75 us
    all_to_all x1, waiting for transfers between devices: 26.4 us -> 2.97 us  [on_device(): lax.all_to_all(picked, ('x', 'zl'), split_axis=0, concat_axis=0, tiled=True)]
    ppermute x1 -> x5, starting transfers between devices: 3.14 us -> 22.1 us  [the longest x3 10.7 us: on_device(): lax.ppermute(block, 'y', [(y, (y + step) % Y) for y in range(Y)])]
    all_to_all x1, starting transfers between devices: 11.9 us -> 3.73 us  [on_device(): lax.all_to_all(picked, ('x', 'zl'), split_axis=0, concat_axis=0, tiled=True)]
    unnamed x8 -> x14, local copies, waits for them, and re-layouts: 2.41 us -> 4.64 us
    all_to_all x1, blocking collectives: 9.4 us -> 11.6 us  [on_device(): lax.all_to_all(packed, ('x', 'zl'), split_axis=0, concat_axis=0, tiled=True)]
    ppermute x1 -> x5, waiting for transfers between devices: 6.84 us -> 6.15 us  [the longest x3 3.79 us: on_device(): lax.ppermute(block, 'y', [(y, (y + step) % Y) for y in range(Y)])]
    pallas_call x2 -> x6, Pallas kernels: 5.06 us -> 4.94 us  [the longest x4 2.41 us: on_device(): pl.pallas_call(mask_kernel, out_shape=jax.ShapeDtypeStruct((2, TILE, MT),...]
  transfers between devices with their start and end apart: 3 -> 6, of which waited for: 2 -> 4; matrix products, arithmetic and copies ran while one was open for 0% -> 0% of each run, Pallas kernels for 4% -> 2%
where the time goes in v2:
time: 115 us; the launch traced here: 114 us
  blocking collectives  63.7 us (55%)
  starting transfers between devices  25.9 us (23%)
  Pallas kernels  9.77 us (8%)
  waiting for transfers between devices  9.12 us (8%)
  local copies, waits for them, and re-layouts  4.75 us (4%)
    all_gather x1, blocking collectives, on_device(): own = lax.all_gather(spread[:, :SLICE], 'zh', axis=0, tiled=True)  31.6 us
    all_to_all x1, blocking collectives, on_device(): lax.all_to_all(terms, ('y', 'c'), split_axis=0, concat_axis=0, tiled=True)  20.5 us
    all_to_all x1, blocking collectives, on_device(): lax.all_to_all(packed, ('x', 'zl'), split_axis=0, concat_axis=0, tiled=True)  11.6 us
    ppermute x3, starting transfers between devices, on_device(): lax.ppermute(block, 'y', [(y, (y + step) % Y) for y in range(Y)])  10.7 us
    ppermute x1, starting transfers between devices, on_device(): other = lax.ppermute(own, 'c', [(0, 1), (1, 0)])  9.14 us
    pallas_call x1, Pallas kernels, on_device(): pl.pallas_call(ladder_kernel, out_shape=jax.ShapeDtypeStruct((Y * C, rows...  4.83 us
    unnamed x14, local copies, waits for them, and re-layouts  4.64 us
    ppermute x3, waiting for transfers between devices, on_device(): lax.ppermute(block, 'y', [(y, (y + step) % Y) for y in range(Y)])  3.79 us
  transfers between devices with their start and end apart: 6, of which 4 were waited for; matrix products, arithmetic and copies ran while one was open for 0% of the time, Pallas kernels for 2%

profile of v2, /device:TPU:1, one launch (start us, length us, event | category | flops | bytes accessed | tf_op | source)
XLA Modules:
  0.0 114.3 jit_solution(9619475441347501327)
XLA Ops:
  0.0 1.5 %shard_map.55 = f32[8,24,128]{2,1,0:T(8,128)} custom-call(s32[2,4]{1,0:T(2,128)} %domains.1, s32[64]{0:T(128)} %owner_map.1, f32[128,128]{1,0:T(8,128)} %bitcast.12), custom_call_target="tpu_custom_call" | custom-call | tf_op jit(solution)/shard_map/pallas_call | solution.py:113
  1.5 11.6 %all_to_all.15 = f32[8,24,128]{2,1,0:T(8,128)S(1)} all-to-all(f32[8,24,128]{2,1,0:T(8,128)} %shard_map.55), channel_id=1, replica_groups=mesh['x'=4,'zh'=8,'zl'=2,'y'=4,'c'=2] {'x','zl'}, dimensions={0} | all-to-all | bytes 196608 | tf_op jit(solution)/shard_map/all_to_all | solution.py:119
  13.1 31.6 %all_gather.3.own = f32[64,16,128]{2,1,0:T(8,128)S(1)} all-gather(f32[8,16,128]{2,1,0:T(8,128)S(1)} %slice.9), channel_id=1, replica_groups=mesh['x'=4,'zh'=8,'zl'=2,'y'=4,'c'=2] {'zh'}, dimensions={0}, use_global_device_ids=true | all-gather | bytes 589824 | tf_op jit(solution)/shard_map/all_gather | solution.py:121
  44.7 9.1 %collective-permute-start = (f32[64,16,128]{2,1,0:T(8,128)S(1)}, f32[64,16,128]{2,1,0:T(8,128)S(1)}, u32[]{:S(2)}, u32[]{:S(2)}) collective-permute-start(f32[64,16,128]{2,1,0:T(8,128)S(1)} %all_gather.3.own), channel_id=1, source_target_pairs={{0,1},{1,0},{2,3},{3,2},{4,5},{5,4},{6,7},{7,6},{8,9},{9,8},{10,11... | collective-permute-start | bytes 1572872 | tf_op jit(solution)/shard_map/ppermute | solution.py:122
  53.9 0.1 convert_element_type.8.wanted
  54.0 1.4 %collective-permute-done.other = f32[64,16,128]{2,1,0:T(8,128)S(1)} collective-permute-done((f32[64,16,128]{2,1,0:T(8,128)S(1)}, f32[64,16,128]{2,1,0:T(8,128)S(1)}, u32[]{:S(2)}, u32[]{:S(2)}) %collective-permute-start) | collective-permute-done | bytes 524320 | tf_op jit(solution)/shard_map/ppermute | solution.py:122
  55.4 1.0 shard_map.56
  56.4 0.0 copy-start
  56.4 1.3 %copy-done = f32[8,2,16,16,128]{4,3,2,1,0:T(8,128)} copy-done((f32[8,2,16,16,128]{4,3,2,1,0:T(8,128)}, f32[8,2,16,16,128]{4,3,2,1,0:T(8,128)S(1)}, u32[]{:S(2)}) %copy-start) | copy-done | bytes 2097176
  57.7 0.0 copy-start.6
  57.7 0.0 copy-start.5
  57.8 3.7 %all-to-all-start.1 = ((f32[8,2,16,16,128]{4,3,2,1,0:T(8,128)}), f32[8,2,16,16,128]{4,3,2,1,0:T(8,128)S(1)}, u32[]{:S(2)}, u32[]{:S(2)}) async-start(f32[8,2,16,16,128]{4,3,2,1,0:T(8,128)} %copy-done), calls=%async_computation.1 | async-start | bytes 4194304 | tf_op jit(solution)/shard_map/all_to_all | solution.py:132
  61.5 0.0 copy-done.6
  61.5 2.3 %collective-permute-start.1 = (f32[64,512]{1,0:T(8,128)S(1)}, f32[64,512]{1,0:T(8,128)S(1)}, u32[]{:S(2)}, u32[]{:S(2)}) collective-permute-start(f32[64,512]{1,0:T(8,128)S(1)} %get-tuple-element.10), channel_id=1, source_target_pairs={{0,1},{1,0},{2,3},{3,2},{4,5},{5,4},{6,7},{7,6},{8,9},{9,8},{10,11... | collective-permute-start | bytes 393224 | tf_op jit(solution)/shard_map/ppermute | solution.py:136
  63.8 1.0 collective-permute-done.1
  64.8 3.2 %collective-permute-start.2 = (f32[128,512]{1,0:T(8,128)S(1)}, f32[128,512]{1,0:T(8,128)S(1)}, u32[]{:S(2)}, u32[]{:S(2)}) collective-permute-start(f32[128,512]{1,0:T(8,128)S(1)} %maximum_select_fusion.amps), channel_id=1, source_target_pairs={{0,2},{2,4},{4,6},{6,0},{1,3},{3,5},{5,7},{7,1},{8,10},{10,12},{12... | collective-permute-start | bytes 786440 | tf_op jit(solution)/shard_map/ppermute | solution.py:140
  68.0 4.5 %collective-permute-start.3 = (f32[128,512]{1,0:T(8,128)S(1)}, f32[128,512]{1,0:T(8,128)S(1)}, u32[]{:S(2)}, u32[]{:S(2)}) collective-permute-start(f32[128,512]{1,0:T(8,128)S(1)} %maximum_select_fusion.amps), channel_id=1, source_target_pairs={{0,4},{2,6},{4,0},{6,2},{1,5},{3,7},{5,1},{7,3},{8,12},{10,14},{12... | collective-permute-start | bytes 786440 | tf_op jit(solution)/shard_map/ppermute | solution.py:140
  72.6 3.0 %collective-permute-start.4 = (f32[128,512]{1,0:T(8,128)S(1)}, f32[128,512]{1,0:T(8,128)S(1)}, u32[]{:S(2)}, u32[]{:S(2)}) collective-permute-start(f32[128,512]{1,0:T(8,128)S(1)} %maximum_select_fusion.amps), channel_id=1, source_target_pairs={{0,6},{2,0},{4,2},{6,4},{1,7},{3,1},{5,3},{7,5},{8,14},{10,8},{12,... | collective-permute-start | bytes 786440 | tf_op jit(solution)/shard_map/ppermute | solution.py:140
  75.6 0.1 pad_add_fusion.places
  75.6 0.0 copy-done.5
  75.6 0.6 shard_map.57.m0
  76.3 0.0 collective-permute-done.2.amps
  76.3 0.0 copy-start.3
  76.3 0.7 copy-done.3
  77.0 0.0 copy-start.4
  77.0 0.9 copy-done.4
  77.9 0.6 shard_map.58.m1
  78.5 3.8 %collective-permute-done.3.amps = f32[128,512]{1,0:T(8,128)S(1)} collective-permute-done((f32[128,512]{1,0:T(8,128)S(1)}, f32[128,512]{1,0:T(8,128)S(1)}, u32[]{:S(2)}, u32[]{:S(2)}) %collective-permute-start.3) | collective-permute-done | bytes 262176 | tf_op jit(solution)/shard_map/ppermute | solution.py:140
  82.3 0.0 copy-start.1
  82.3 0.7 copy-done.1
  83.0 0.0 copy-start.2
  83.0 0.9 copy-done.2
  84.0 0.6 shard_map.59.m2
  84.6 0.0 collective-permute-done.4.amps
  84.6 0.6 shard_map.60.m3
  85.2 3.0 %all-to-all-done.1.tiles = f32[8,2,16,16,128]{4,3,2,1,0:T(8,128)S(1)} async-done(((f32[8,2,16,16,128]{4,3,2,1,0:T(8,128)}), f32[8,2,16,16,128]{4,3,2,1,0:T(8,128)S(1)}, u32[]{:S(2)}, u32[]{:S(2)}) %all-to-all-start.1) | async-done | bytes 2097184 | tf_op jit(solution)/shard_map/all_to_all | solution.py:132
  88.2 4.8 %shard_map.61 = f32[8,64,512]{2,1,0:T(8,128)S(1)} custom-call(s32[1]{0:T(128)} %bitcast.core, s32[4]{0:T(128)S(1)} %pad_add_fusion.places, s32[2]{0:T(128)S(1)} %copy-done.5, f32[8,2,16,16,128]{4,3,2,1,0:T(8,128)S(1)} %all-to-all-done.1.tiles, bf16[2,128,512]{2,1,0:T(8,128)(2,1)S(1)} %shard_map.57.m0, bf16[2,128,512]{2,1,0:T(8,128)(2,1)S(1)} %shard_map.58.m1, ...), custom_call_target="tpu_custom_call" | custom-call | tf_op jit(solution)/shard_map/pallas_call | solution.py:153
  93.0 20.5 %all_to_all.16 = f32[8,64,512]{2,1,0:T(8,128)S(1)} all-to-all(f32[8,64,512]{2,1,0:T(8,128)S(1)} %shard_map.61), channel_id=1, replica_groups=mesh['x'=4,'zh'=8,'zl'=2,'y'=4,'c'=2] {'y','c'}, dimensions={0} | all-to-all | bytes 2097152 | tf_op jit(solution)/shard_map/all_to_all | solution.py:166
  113.5 0.8 reduce_sum.9
  (4 shorter events, 0.1 us)
Async XLA Ops:
  44.7 10.7 %collective-permute-start = (f32[64,16,128]{2,1,0:T(8,128)S(1)}, f32[64,16,128]{2,1,0:T(8,128)S(1)}, u32[]{:S(2)}, u32[]{:S(2)}) collective-permute-start(f32[64,16,128]{2,1,0:T(8,128)S(1)} %all_gather.3.own), channel_id=1, source_target_pairs={{0,1},{1,0},{2,3},{3,2},{4,5},{5,4},{6,7},{7,6},{8,9},{9,8},{10,11... | collective-permute-start | bytes 1572872 | tf_op jit(solution)/shard_map/ppermute | solution.py:122
  56.4 1.3 %copy-start = (f32[8,2,16,16,128]{4,3,2,1,0:T(8,128)}, f32[8,2,16,16,128]{4,3,2,1,0:T(8,128)S(1)}, u32[]{:S(2)}) copy-start(f32[8,2,16,16,128]{4,3,2,1,0:T(8,128)S(1)} %shard_map.56) | copy-start | bytes 6291460
  57.7 3.8 %copy-start.6 = (f32[2,64,512]{2,1,0:T(8,128)S(1)}, f32[2,64,512]{2,1,0:T(8,128)}, u32[]{:S(2)}) copy-start(f32[2,64,512]{2,1,0:T(8,128)} %param.5) | copy-start | bytes 786436
  57.7 17.9 %copy-start.5 = (s32[2]{0:T(128)S(1)}, s32[2]{0:T(128)}, u32[]{:S(2)}) copy-start(s32[2]{0:T(128)} %lengths.9) | copy-start | bytes 28
  57.8 30.4 %all-to-all-start.1 = ((f32[8,2,16,16,128]{4,3,2,1,0:T(8,128)}), f32[8,2,16,16,128]{4,3,2,1,0:T(8,128)S(1)}, u32[]{:S(2)}, u32[]{:S(2)}) async-start(f32[8,2,16,16,128]{4,3,2,1,0:T(8,128)} %copy-done), calls=%async_computation.1 | async-start | bytes 4194304 | tf_op jit(solution)/shard_map/all_to_all | solution.py:132
  61.5 3.3 %collective-permute-start.1 = (f32[64,512]{1,0:T(8,128)S(1)}, f32[64,512]{1,0:T(8,128)S(1)}, u32[]{:S(2)}, u32[]{:S(2)}) collective-permute-start(f32[64,512]{1,0:T(8,128)S(1)} %get-tuple-element.10), channel_id=1, source_target_pairs={{0,1},{1,0},{2,3},{3,2},{4,5},{5,4},{6,7},{7,6},{8,9},{9,8},{10,11... | collective-permute-start | bytes 393224 | tf_op jit(solution)/shard_map/ppermute | solution.py:136
  64.8 11.4 %collective-permute-start.2 = (f32[128,512]{1,0:T(8,128)S(1)}, f32[128,512]{1,0:T(8,128)S(1)}, u32[]{:S(2)}, u32[]{:S(2)}) collective-permute-start(f32[128,512]{1,0:T(8,128)S(1)} %maximum_select_fusion.amps), channel_id=1, source_target_pairs={{0,2},{2,4},{4,6},{6,0},{1,3},{3,5},{5,7},{7,1},{8,10},{10,12},{12... | collective-permute-start | bytes 786440 | tf_op jit(solution)/shard_map/ppermute | solution.py:140
  68.0 14.3 %collective-permute-start.3 = (f32[128,512]{1,0:T(8,128)S(1)}, f32[128,512]{1,0:T(8,128)S(1)}, u32[]{:S(2)}, u32[]{:S(2)}) collective-permute-start(f32[128,512]{1,0:T(8,128)S(1)} %maximum_select_fusion.amps), channel_id=1, source_target_pairs={{0,4},{2,6},{4,0},{6,2},{1,5},{3,7},{5,1},{7,3},{8,12},{10,14},{12... | collective-permute-start | bytes 786440 | tf_op jit(solution)/shard_map/ppermute | solution.py:140
  72.6 12.0 %collective-permute-start.4 = (f32[128,512]{1,0:T(8,128)S(1)}, f32[128,512]{1,0:T(8,128)S(1)}, u32[]{:S(2)}, u32[]{:S(2)}) collective-permute-start(f32[128,512]{1,0:T(8,128)S(1)} %maximum_select_fusion.amps), channel_id=1, source_target_pairs={{0,6},{2,0},{4,2},{6,4},{1,7},{3,1},{5,3},{7,5},{8,14},{10,8},{12,... | collective-permute-start | bytes 786440 | tf_op jit(solution)/shard_map/ppermute | solution.py:140
  76.3 0.7 copy-start.3
  77.0 0.9 copy-start.4
  82.3 0.7 copy-start.1
  83.0 0.9 copy-start.2

commit v3 on v2

v3 whole, which is shorter than its diff:
```python
import jax
import jax.numpy as jnp
from jax import lax
from jax.experimental import pallas as pl
from jax.experimental.pallas import tpu as pltpu
from jax.sharding import Mesh, PartitionSpec as P

TILE = 128
M = 4
NT = 8
MT = M * TILE
X, ZH, ZL, Y, C = 4, 8, 2, 4, 2
G = X * ZL
SLICE = TILE // G
KINDS = M * M
f32, bf16 = jnp.float32, jnp.bfloat16
VMEM = pl.BlockSpec(memory_space=pltpu.VMEM)
SMALL = pltpu.CompilerParams(vmem_limit_bytes=16 * 2**20)
SMEM = pl.BlockSpec(memory_space=pltpu.SMEM)
ANY = pl.BlockSpec(memory_space=pl.ANY)


def pack_kernel(core, plane, domains, lengths, owner_map, store, out, mask):
    lane = lax.broadcasted_iota(jnp.int32, (8, TILE), 1)
    wanted = jnp.zeros((8, TILE), jnp.int32)
    for p in range(C):
        for a in range(M):
            for c in range(M):
                place = owner_map[domains[p, a] * NT + domains[p, c]]
                wanted = jnp.where(lane == p * KINDS + a * M + c, place, wanted)
    z = lax.rem(wanted, ZH * ZL)
    wanted = lax.div(z, ZL) * G + lax.rem(z, ZL) * X + lax.div(wanted, ZH * ZL)
    wanted = wanted.astype(f32)
    for g in range(G):
        out[g, :SLICE, :] = store[g * SLICE:(g + 1) * SLICE, :]
        out[g, SLICE:, :] = wanted
    length = lengths[core[0]]
    step = lax.broadcasted_iota(jnp.int32, (8, MT), 0)
    column = lax.broadcasted_iota(jnp.int32, (8, MT), 1)
    tile = lax.rem(plane[0] + 2 * Y - step, Y)
    mask[...] = jnp.where((tile < length) & (column < length * TILE), 1.0, 0.0).astype(f32)


def pick_kernel(wanted, core, own, other, out, held, sems):
    first = core[0] * KINDS
    copies = []
    for g in range(G):
        for k in range(KINDS):
            row = wanted[g * C * KINDS + first + k]
            held[g, 0, k] = own[row]
            held[g, 1, k] = other[row]
        copies.append(pltpu.make_async_copy(held.at[g], out.at[g], sems.at[g]))
        copies[-1].start()
    for copy in copies:
        copy.wait()


def split(value):
    high = value.astype(bf16)
    return high, (value - high.astype(f32)).astype(bf16)


def product(left, right, dims):
    def one(a, b):
        return lax.dot_general(a, b, (dims, ((), ())), preferred_element_type=f32)

    return one(left[0], right[0]) + (one(left[0], right[1]) + one(left[1], right[0]))


def live_tiles(core, lengths):
    length = lengths[core[0]]
    return [jnp.where(a < length, 1.0, 0.0).astype(f32) for a in range(M)]


def ladder_kernel(core, places, lengths, tiles, *refs):
    parts, (out, d_high, d_low, t_high, t_low) = refs[:2 * Y], refs[2 * Y:]
    for i, part in enumerate(parts):
        rows = pl.ds(pl.multiple_of(places[i // 2] * TILE, TILE), TILE)
        (t_high, t_low)[i % 2][rows] = part[...]
    live = live_tiles(core, lengths)
    for q in range(C):
        for a in range(M):
            for c in range(M):
                keep = live[a] * live[c]
                for g in range(G):
                    at = a * TILE + g * SLICE
                    at = (q, slice(at, at + SLICE), slice(c * TILE, (c + 1) * TILE))
                    d_high[at], d_low[at] = split(tiles[g, q, a * M + c] * keep)
    rows = MT // (Y * C)
    for r in range(2):
        at = slice(r * 256, (r + 1) * 256)
        total = None
        for q in range(C):
            half = product((d_high[q, at], d_low[q, at]), (t_high[...], t_low[...]), ((1,), (0,)))
            term = product(split(half), (d_high[q], d_low[q]), ((1,), (1,)))
            total = term if total is None else total + term
        for v in range(r * Y, (r + 1) * Y):
            out[v % C * Y + v // C] = total[(v - r * Y) * rows:(v + 1 - r * Y) * rows]


def on_device(amplitudes, integral_store, domains, domain_length, owner_map):
    pairs, rows, _ = amplitudes.shape
    core = lax.axis_index("c").astype(jnp.int32).reshape(1)
    plane = lax.axis_index("y").astype(jnp.int32).reshape(1)

    packed, mask = pl.pallas_call(
        pack_kernel,
        out_shape=[
            jax.ShapeDtypeStruct((G, SLICE + 8, TILE), f32),
            jax.ShapeDtypeStruct((8, MT), f32),
        ],
        in_specs=[SMEM] * 5 + [VMEM],
        out_specs=[VMEM, VMEM],
    )(core, plane, domains, domain_length, owner_map, integral_store.reshape(TILE, TILE))
    spread = lax.all_to_all(packed, ("zl", "x"), split_axis=0, concat_axis=0, tiled=True)
    wanted = spread[:, SLICE, :pairs * KINDS].astype(jnp.int32).reshape(-1)
    own = lax.all_gather(spread[:, :SLICE], "zh", axis=0, tiled=True)
    other = lax.ppermute(own, "c", [(0, 1), (1, 0)])
    picked = pl.pallas_call(
        pick_kernel,
        out_shape=pltpu.HBM((G, C, KINDS, SLICE, TILE), f32),
        in_specs=[SMEM, SMEM, VMEM, VMEM],
        out_specs=pl.BlockSpec(memory_space=pltpu.HBM),
        scratch_shapes=[pltpu.VMEM((G, C, KINDS, SLICE, TILE), f32), pltpu.SemaphoreType.DMA((G,))],
        compiler_params=SMALL,
    )(wanted, core, own, other)
    picked, amplitudes = lax.optimization_barrier((picked, amplitudes))
    tiles = lax.all_to_all(picked, ("zl", "x"), split_axis=0, concat_axis=0, tiled=True)

    mine = lax.axis_index("c")
    given = lax.dynamic_index_in_dim(amplitudes, 1 - mine, 0, keepdims=False)
    got = lax.ppermute(given, "c", [(0, 1), (1, 0)])
    kept = lax.dynamic_index_in_dim(amplitudes, mine, 0, keepdims=False)
    block = jnp.where(mine == 0, jnp.concatenate([kept, got]), jnp.concatenate([got, kept]))
    before, across, after = (
        lax.ppermute(block, "y", [(y, (y + step) % Y) for y in range(Y)]) for step in (1, 2, 3)
    )
    places = jnp.concatenate([lax.rem(plane + Y - step, Y) for step in range(Y)])
    masked = []
    for step, part in enumerate((block, before, across, after)):
        value = part * mask[step:step + 1]
        high = lax.reduce_precision(value, 8, 7)
        masked += [high.astype(bf16), (value - high).astype(bf16)]
    terms = pl.pallas_call(
        ladder_kernel,
        out_shape=jax.ShapeDtypeStruct((Y * C, rows, MT), f32),
        in_specs=[SMEM, SMEM, SMEM, VMEM] + [VMEM] * (2 * Y),
        out_specs=VMEM,
        scratch_shapes=[
            pltpu.VMEM((C, MT, MT), bf16),
            pltpu.VMEM((C, MT, MT), bf16),
            pltpu.VMEM((MT, MT), bf16),
            pltpu.VMEM((MT, MT), bf16),
        ],
        compiler_params=pltpu.CompilerParams(vmem_limit_bytes=24 * 2**20),
    )(core, places, domain_length, tiles, *masked)
    parts = lax.all_to_all(terms, ("c", "y"), split_axis=0, concat_axis=0, tiled=True)
    return parts.reshape(pairs, Y, rows, MT).sum(1)


def solution(mesh):
    cut = Mesh(mesh.devices.reshape(X, ZH, ZL, Y, C), ("x", "zh", "zl", "y", "c"))
    pair, virt = ("x", "zh", "zl"), ("y", "c")
    placed = (
        P(pair, virt, None),
        P(virt, pair, None, None),
        P(pair, None),
        P(pair),
        P(),
    )
    return jax.shard_map(
        on_device, mesh=cut, in_specs=placed, out_specs=P(pair, virt, None), check_vma=False
    )
```

time: 115 us -> 113 us (0.983)
  waiting for transfers between devices: 9.12 us -> 15.3 us
  local copies, waits for them, and re-layouts: 4.75 us -> 0.13 us
  Pallas kernels: 9.77 us -> 7.87 us
    ppermute x3, waiting for transfers between devices: 3.79 us -> 12.2 us  [on_device(): lax.ppermute(block, 'y', [(y, (y + step) % Y) for y in range(Y)])]
    unnamed x14 -> x6, local copies, waits for them, and re-layouts: 4.64 us -> 0.02 us
    all_to_all x1, waiting for transfers between devices: 2.97 us -> 0.75 us  [on_device(): lax.all_to_all(picked, ('zl', 'x'), split_axis=0, concat_axis=0, tiled=True)]
    pallas_call x6 -> x2, Pallas kernels: 4.94 us -> 3.51 us  [the longest x1 1.97 us: on_device(): pl.pallas_call(pick_kernel, out_shape=pltpu.HBM((G, C, KINDS, SLICE, TILE...]
    ppermute x3, starting transfers between devices: 10.7 us -> 9.49 us  [on_device(): lax.ppermute(block, 'y', [(y, (y + step) % Y) for y in range(Y)])]
  transfers between devices with their start and end apart: 6 -> 6, of which waited for: 4 -> 5; matrix products, arithmetic and copies ran while one was open for 0% -> 0% of each run, Pallas kernels for 2% -> 0%
where the time goes in v3:
time: 113 us
  blocking collectives  63 us (56%)
  starting transfers between devices  25.1 us (22%)
  waiting for transfers between devices  15.3 us (14%)
  Pallas kernels  7.87 us (7%)
    all_gather x1, blocking collectives, on_device(): own = lax.all_gather(spread[:, :SLICE], 'zh', axis=0, tiled=True)  31.5 us
    all_to_all x1, blocking collectives, on_device(): lax.all_to_all(terms, ('c', 'y'), split_axis=0, concat_axis=0, tiled=True)  20 us
    ppermute x3, waiting for transfers between devices, on_device(): lax.ppermute(block, 'y', [(y, (y + step) % Y) for y in range(Y)])  12.2 us
    all_to_all x1, blocking collectives, on_device(): lax.all_to_all(packed, ('zl', 'x'), split_axis=0, concat_axis=0, tiled=True)  11.5 us
    ppermute x1, starting transfers between devices, on_device(): other = lax.ppermute(own, 'c', [(0, 1), (1, 0)])  9.63 us
    ppermute x3, starting transfers between devices, on_device(): lax.ppermute(block, 'y', [(y, (y + step) % Y) for y in range(Y)])  9.49 us
    pallas_call x1, Pallas kernels, on_device(): pl.pallas_call(ladder_kernel, out_shape=jax.ShapeDtypeStruct((Y * C, rows...  4.36 us
    all_to_all x1, starting transfers between devices, on_device(): lax.all_to_all(picked, ('zl', 'x'), split_axis=0, concat_axis=0, tiled=True)  3.75 us
  transfers between devices with their start and end apart: 6, of which 5 were waited for; matrix products, arithmetic and copies ran while one was open for 0% of the time, Pallas kernels for 0%

profile of v3, /device:TPU:1, one launch (start us, length us, event | category | flops | bytes accessed | tf_op | source)
XLA Modules:
  0.0 112.7 jit_solution(15718129016856610831)
XLA Ops:
  0.0 1.5 %shard_map.55 = (f32[8,24,128]{2,1,0:T(8,128)}, f32[8,512]{1,0:T(8,128)}) custom-call(s32[1]{0:T(128)} %bitcast.core, s32[1]{0:T(128)} %bitcast.1.plane, s32[2,4]{1,0:T(2,128)} %domains.1, s32[2]{0:T(128)} %lengths.3, s32[64]{0:T(128)} %owner_map.1, f32[128,128]{1,0:T(8,128)} %bitcast.13), custom_call_target="tpu_custom_call" | custom-call | tf_op jit(solution)/shard_map/pallas_call | solution.py:106
  1.5 11.5 %all_to_all.15 = f32[8,24,128]{2,1,0:T(8,128)S(1)} all-to-all(f32[8,24,128]{2,1,0:T(8,128)} %get-tuple-element.9), channel_id=1, replica_groups=mesh['x'=4,'zh'=8,'zl'=2,'y'=4,'c'=2] {'zl','x'}, dimensions={0} | all-to-all | bytes 196608 | tf_op jit(solution)/shard_map/all_to_all | solution.py:115
  13.0 31.5 %all_gather.3.own = f32[64,16,128]{2,1,0:T(8,128)S(1)} all-gather(f32[8,16,128]{2,1,0:T(8,128)S(1)} %slice.25), channel_id=1, replica_groups=mesh['x'=4,'zh'=8,'zl'=2,'y'=4,'c'=2] {'zh'}, dimensions={0}, use_global_device_ids=true | all-gather | bytes 589824 | tf_op jit(solution)/shard_map/all_gather | solution.py:117
  44.5 9.6 %collective-permute-start = (f32[64,16,128]{2,1,0:T(8,128)S(1)}, f32[64,16,128]{2,1,0:T(8,128)S(1)}, u32[]{:S(2)}, u32[]{:S(2)}) collective-permute-start(f32[64,16,128]{2,1,0:T(8,128)S(1)} %all_gather.3.own), channel_id=1, source_target_pairs={{0,1},{1,0},{2,3},{3,2},{4,5},{5,4},{6,7},{7,6},{8,9},{9,8},{10,11... | collective-permute-start | bytes 1572872 | tf_op jit(solution)/shard_map/ppermute | solution.py:118
  54.2 0.1 convert_element_type.32.wanted
  54.2 1.4 %collective-permute-done.other = f32[64,16,128]{2,1,0:T(8,128)S(1)} collective-permute-done((f32[64,16,128]{2,1,0:T(8,128)S(1)}, f32[64,16,128]{2,1,0:T(8,128)S(1)}, u32[]{:S(2)}, u32[]{:S(2)}) %collective-permute-start) | collective-permute-done | bytes 524320 | tf_op jit(solution)/shard_map/ppermute | solution.py:118
  55.7 2.0 %shard_map.56 = f32[8,2,16,16,128]{4,3,2,1,0:T(8,128)} custom-call(s32[256]{0:T(256)S(1)} %convert_element_type.32.wanted, s32[1]{0:T(128)} %bitcast.core, f32[64,16,128]{2,1,0:T(8,128)S(1)} %all_gather.3.own, f32[64,16,128]{2,1,0:T(8,128)S(1)} %collective-permute-done.other), custom_call_target="tpu_custom_call" | custom-call | tf_op jit(solution)/shard_map/pallas_call | solution.py:119
  57.6 0.0 copy-start.1
  57.7 0.0 copy-start.2
  57.7 3.7 %all-to-all-start.1 = ((f32[8,2,16,16,128]{4,3,2,1,0:T(8,128)}), f32[8,2,16,16,128]{4,3,2,1,0:T(8,128)S(1)}, u32[]{:S(2)}, u32[]{:S(2)}) async-start(f32[8,2,16,16,128]{4,3,2,1,0:T(8,128)} %shard_map.56), calls=%async_computation.1 | async-start | bytes 4194304 | tf_op jit(solution)/shard_map/all_to_all | solution.py:128
  61.4 0.0 copy-start
  61.4 0.0 copy-done.1
  61.5 2.3 %collective-permute-start.1 = (f32[64,512]{1,0:T(8,128)S(1)}, f32[64,512]{1,0:T(8,128)S(1)}, u32[]{:S(2)}, u32[]{:S(2)}) collective-permute-start(f32[64,512]{1,0:T(8,128)S(1)} %get-tuple-element.21), channel_id=1, source_target_pairs={{0,1},{1,0},{2,3},{3,2},{4,5},{5,4},{6,7},{7,6},{8,9},{9,8},{10,11... | collective-permute-start | bytes 393224 | tf_op jit(solution)/shard_map/ppermute | solution.py:132
  63.8 0.0 copy-done.2
  63.8 0.9 collective-permute-done.1
  64.8 4.6 %collective-permute-start.4 = (f32[128,512]{1,0:T(8,128)S(1)}, f32[128,512]{1,0:T(8,128)S(1)}, u32[]{:S(2)}, u32[]{:S(2)}) collective-permute-start(f32[128,512]{1,0:T(8,128)S(1)} %get-tuple-element.14), channel_id=1, source_target_pairs={{0,6},{2,0},{4,2},{6,4},{1,7},{3,1},{5,3},{7,5},{8,14},{10,8},{12,... | collective-permute-start | bytes 786440 | tf_op jit(solution)/shard_map/ppermute | solution.py:136
  69.4 0.1 pad_add_fusion.places
  69.5 2.2 %collective-permute-start.3 = (f32[128,512]{1,0:T(8,128)S(1)}, f32[128,512]{1,0:T(8,128)S(1)}, u32[]{:S(2)}, u32[]{:S(2)}) collective-permute-start(f32[128,512]{1,0:T(8,128)S(1)} %get-tuple-element.14), channel_id=1, source_target_pairs={{0,4},{2,6},{4,0},{6,2},{1,5},{3,7},{5,1},{7,3},{8,12},{10,14},{12... | collective-permute-start | bytes 786440 | tf_op jit(solution)/shard_map/ppermute | solution.py:136
  71.8 2.6 %collective-permute-start.2 = (f32[128,512]{1,0:T(8,128)S(1)}, f32[128,512]{1,0:T(8,128)S(1)}, u32[]{:S(2)}, u32[]{:S(2)}) collective-permute-start(f32[128,512]{1,0:T(8,128)S(1)} %get-tuple-element.14), channel_id=1, source_target_pairs={{0,2},{2,4},{4,6},{6,0},{1,3},{3,5},{5,7},{7,1},{8,10},{10,12},{12... | collective-permute-start | bytes 786440 | tf_op jit(solution)/shard_map/ppermute | solution.py:136
  74.4 5.8 %collective-permute-done.4 = f32[128,512]{1,0:T(8,128)S(1)} collective-permute-done((f32[128,512]{1,0:T(8,128)S(1)}, f32[128,512]{1,0:T(8,128)S(1)}, u32[]{:S(2)}, u32[]{:S(2)}) %collective-permute-start.4) | collective-permute-done | bytes 262176 | tf_op jit(solution)/shard_map/ppermute | solution.py:136
  80.3 0.0 collective-permute-done.3
  80.3 6.4 %collective-permute-done.2 = f32[128,512]{1,0:T(8,128)S(1)} collective-permute-done((f32[128,512]{1,0:T(8,128)S(1)}, f32[128,512]{1,0:T(8,128)S(1)}, u32[]{:S(2)}, u32[]{:S(2)}) %collective-permute-start.2) | collective-permute-done | bytes 262176 | tf_op jit(solution)/shard_map/ppermute | solution.py:136
  86.8 0.8 all-to-all-done.1.tiles
  87.6 0.0 copy-done
  87.6 4.4 %shard_map.57 = f32[8,64,512]{2,1,0:T(8,128)S(1)} custom-call(s32[1]{0:T(128)} %bitcast.core, s32[4]{0:T(128)S(1)} %pad_add_fusion.places, s32[2]{0:T(128)S(1)} %copy-done, f32[8,2,16,16,128]{4,3,2,1,0:T(8,128)S(1)} %all-to-all-done.1.tiles, bf16[128,512]{1,0:T(8,128)(2,1)S(1)} %reduce-precision_convert_fusion.3.refs_0_, ...), custom_call_target="tpu_custom_call" | custom-call | tf_op jit(solution)/shard_map/pallas_call | solution.py:144
  91.9 20.0 %all_to_all.16 = f32[8,64,512]{2,1,0:T(8,128)S(1)} all-to-all(f32[8,64,512]{2,1,0:T(8,128)S(1)} %shard_map.57), channel_id=1, replica_groups=mesh['x'=4,'zh'=8,'zl'=2,'y'=4,'c'=2] {'c','y'}, dimensions={0} | all-to-all | bytes 2097152 | tf_op jit(solution)/shard_map/all_to_all | solution.py:157
  111.9 0.8 bitcast_reduce_fusion
  (9 shorter events, 0.3 us)
Async XLA Ops:
  44.5 11.2 %collective-permute-start = (f32[64,16,128]{2,1,0:T(8,128)S(1)}, f32[64,16,128]{2,1,0:T(8,128)S(1)}, u32[]{:S(2)}, u32[]{:S(2)}) collective-permute-start(f32[64,16,128]{2,1,0:T(8,128)S(1)} %all_gather.3.own), channel_id=1, source_target_pairs={{0,1},{1,0},{2,3},{3,2},{4,5},{5,4},{6,7},{7,6},{8,9},{9,8},{10,11... | collective-permute-start | bytes 1572872 | tf_op jit(solution)/shard_map/ppermute | solution.py:118
  57.6 3.8 %copy-start.1 = (f32[2,64,512]{2,1,0:T(8,128)S(1)}, f32[2,64,512]{2,1,0:T(8,128)}, u32[]{:S(2)}) copy-start(f32[2,64,512]{2,1,0:T(8,128)} %param.5) | copy-start | bytes 786436
  57.7 6.1 %copy-start.2 = (f32[8,512]{1,0:T(8,128)S(1)}, f32[8,512]{1,0:T(8,128)}, u32[]{:S(2)}) copy-start(f32[8,512]{1,0:T(8,128)} %get-tuple-element.12) | copy-start | bytes 49156
  57.7 29.9 %all-to-all-start.1 = ((f32[8,2,16,16,128]{4,3,2,1,0:T(8,128)}), f32[8,2,16,16,128]{4,3,2,1,0:T(8,128)S(1)}, u32[]{:S(2)}, u32[]{:S(2)}) async-start(f32[8,2,16,16,128]{4,3,2,1,0:T(8,128)} %shard_map.56), calls=%async_computation.1 | async-start | bytes 4194304 | tf_op jit(solution)/shard_map/all_to_all | solution.py:128
  61.4 26.1 %copy-start = (s32[2]{0:T(128)S(1)}, s32[2]{0:T(128)}, u32[]{:S(2)}) copy-start(s32[2]{0:T(128)} %lengths.3) | copy-start | bytes 28
  61.5 3.3 %collective-permute-start.1 = (f32[64,512]{1,0:T(8,128)S(1)}, f32[64,512]{1,0:T(8,128)S(1)}, u32[]{:S(2)}, u32[]{:S(2)}) collective-permute-start(f32[64,512]{1,0:T(8,128)S(1)} %get-tuple-element.21), channel_id=1, source_target_pairs={{0,1},{1,0},{2,3},{3,2},{4,5},{5,4},{6,7},{7,6},{8,9},{9,8},{10,11... | collective-permute-start | bytes 393224 | tf_op jit(solution)/shard_map/ppermute | solution.py:132
  64.8 15.4 %collective-permute-start.4 = (f32[128,512]{1,0:T(8,128)S(1)}, f32[128,512]{1,0:T(8,128)S(1)}, u32[]{:S(2)}, u32[]{:S(2)}) collective-permute-start(f32[128,512]{1,0:T(8,128)S(1)} %get-tuple-element.14), channel_id=1, source_target_pairs={{0,6},{2,0},{4,2},{6,4},{1,7},{3,1},{5,3},{7,5},{8,14},{10,8},{12,... | collective-permute-start | bytes 786440 | tf_op jit(solution)/shard_map/ppermute | solution.py:136
  69.5 10.8 %collective-permute-start.3 = (f32[128,512]{1,0:T(8,128)S(1)}, f32[128,512]{1,0:T(8,128)S(1)}, u32[]{:S(2)}, u32[]{:S(2)}) collective-permute-start(f32[128,512]{1,0:T(8,128)S(1)} %get-tuple-element.14), channel_id=1, source_target_pairs={{0,4},{2,6},{4,0},{6,2},{1,5},{3,7},{5,1},{7,3},{8,12},{10,14},{12... | collective-permute-start | bytes 786440 | tf_op jit(solution)/shard_map/ppermute | solution.py:136
  71.8 14.9 %collective-permute-start.2 = (f32[128,512]{1,0:T(8,128)S(1)}, f32[128,512]{1,0:T(8,128)S(1)}, u32[]{:S(2)}, u32[]{:S(2)}) collective-permute-start(f32[128,512]{1,0:T(8,128)S(1)} %get-tuple-element.14), channel_id=1, source_target_pairs={{0,2},{2,4},{4,6},{6,0},{1,3},{3,5},{5,7},{7,1},{8,10},{10,12},{12... | collective-permute-start | bytes 786440 | tf_op jit(solution)/shard_map/ppermute | solution.py:136

commit v4 on v3

--- a/solution.py
+++ b/solution.py
@@ -41,14 +41,16 @@
     mask[...] = jnp.where((tile < length) & (column < length * TILE), 1.0, 0.0).astype(f32)
 
 
-def pick_kernel(wanted, core, own, other, out, held, sems):
+def pick_kernel(wanted, core, turn, own, other, out, held, sems):
     first = core[0] * KINDS
     copies = []
     for g in range(G):
         for k in range(KINDS):
             row = wanted[g * C * KINDS + first + k]
-            held[g, 0, k] = own[row]
-            held[g, 1, k] = other[row]
+            mine = lax.rem(lax.div(row, G), 2) == turn[0]
+            a, b = own[row], other[row]
+            held[g, 0, k] = jnp.where(mine, a, b)
+            held[g, 1, k] = jnp.where(mine, b, a)
         copies.append(pltpu.make_async_copy(held.at[g], out.at[g], sems.at[g]))
         copies[-1].start()
     for copy in copies:
@@ -87,20 +89,19 @@
                     at = (q, slice(at, at + SLICE), slice(c * TILE, (c + 1) * TILE))
                     d_high[at], d_low[at] = split(tiles[g, q, a * M + c] * keep)
     rows = MT // (Y * C)
-    for r in range(2):
-        at = slice(r * 256, (r + 1) * 256)
-        total = None
-        for q in range(C):
-            half = product((d_high[q, at], d_low[q, at]), (t_high[...], t_low[...]), ((1,), (0,)))
-            term = product(split(half), (d_high[q], d_low[q]), ((1,), (1,)))
-            total = term if total is None else total + term
-        for v in range(r * Y, (r + 1) * Y):
-            out[v % C * Y + v // C] = total[(v - r * Y) * rows:(v + 1 - r * Y) * rows]
+    total = None
+    for q in range(C):
+        half = product((d_high[q], d_low[q]), (t_high[...], t_low[...]), ((1,), (0,)))
+        term = product(split(half), (d_high[q], d_low[q]), ((1,), (1,)))
+        total = term if total is None else total + term
+    for v in range(Y * C):
+        out[v % C * Y + v // C] = total[v * rows:(v + 1) * rows]
 
 
 def on_device(amplitudes, integral_store, domains, domain_length, owner_map):
     pairs, rows, _ = amplitudes.shape
     core = lax.axis_index("c").astype(jnp.int32).reshape(1)
+    turn = lax.rem(lax.axis_index("zh"), 2).astype(jnp.int32).reshape(1)
     plane = lax.axis_index("y").astype(jnp.int32).reshape(1)
 
     packed, mask = pl.pallas_call(
@@ -114,16 +115,17 @@
     )(core, plane, domains, domain_length, owner_map, integral_store.reshape(TILE, TILE))
     spread = lax.all_to_all(packed, ("zl", "x"), split_axis=0, concat_axis=0, tiled=True)
     wanted = spread[:, SLICE, :pairs * KINDS].astype(jnp.int32).reshape(-1)
-    own = lax.all_gather(spread[:, :SLICE], "zh", axis=0, tiled=True)
+    groups = [[C * z + (z + g) % C for z in range(ZH)] for g in range(C)]
+    own = lax.all_gather(spread[:, :SLICE], ("zh", "c"), axis=0, tiled=True, axis_index_groups=groups)
     other = lax.ppermute(own, "c", [(0, 1), (1, 0)])
     picked = pl.pallas_call(
         pick_kernel,
         out_shape=pltpu.HBM((G, C, KINDS, SLICE, TILE), f32),
-        in_specs=[SMEM, SMEM, VMEM, VMEM],
+        in_specs=[SMEM, SMEM, SMEM, VMEM, VMEM],
         out_specs=pl.BlockSpec(memory_space=pltpu.HBM),
         scratch_shapes=[pltpu.VMEM((G, C, KINDS, SLICE, TILE), f32), pltpu.SemaphoreType.DMA((G,))],
         compiler_params=SMALL,
-    )(wanted, core, own, other)
+    )(wanted, core, turn, own, other)
     picked, amplitudes = lax.optimization_barrier((picked, amplitudes))
     tiles = lax.all_to_all(picked, ("zl", "x"), split_axis=0, concat_axis=0, tiled=True)
 

time: 113 us -> 109 us (0.965)
  starting transfers between devices: 25.1 us -> 18.4 us
  blocking collectives: 63 us -> 65.8 us
    ppermute x1, starting transfers between devices: 9.63 us -> 2.85 us  [on_device(): other = lax.ppermute(own, 'c', [(0, 1), (1, 0)])]
    all_gather x1, blocking collectives: 31.5 us -> 34.3 us  [on_device(): lax.all_gather(spread[:, :SLICE], ('zh', 'c'), axis=0, tiled=True, axis_i...]
where the time goes in v4:
time: 109 us; the launch traced here: 108 us
  blocking collectives  65.8 us (60%)
  starting transfers between devices  18.4 us (17%)
  waiting for transfers between devices  15.3 us (14%)
  Pallas kernels  7.62 us (7%)
  other arithmetic  1.09 us (1%)
    all_gather x1, blocking collectives, on_device(): lax.all_gather(spread[:, :SLICE], ('zh', 'c'), axis=0, tiled=True, axis_i...  34.3 us
    all_to_all x1, blocking collectives, on_device(): lax.all_to_all(terms, ('c', 'y'), split_axis=0, concat_axis=0, tiled=True)  20 us
    ppermute x3, waiting for transfers between devices, on_device(): lax.ppermute(block, 'y', [(y, (y + step) % Y) for y in range(Y)])  12.2 us
    all_to_all x1, blocking collectives, on_device(): lax.all_to_all(packed, ('zl', 'x'), split_axis=0, concat_axis=0, tiled=True)  11.5 us
    ppermute x3, starting transfers between devices, on_device(): lax.ppermute(block, 'y', [(y, (y + step) % Y) for y in range(Y)])  9.49 us
    pallas_call x1, Pallas kernels, on_device(): pl.pallas_call(ladder_kernel, out_shape=jax.ShapeDtypeStruct((Y * C, rows...  4.03 us
    all_to_all x1, starting transfers between devices, on_device(): lax.all_to_all(picked, ('zl', 'x'), split_axis=0, concat_axis=0, tiled=True)  3.75 us
    ppermute x1, starting transfers between devices, on_device(): other = lax.ppermute(own, 'c', [(0, 1), (1, 0)])  2.85 us
  transfers between devices with their start and end apart: 6, of which 5 were waited for; matrix products, arithmetic and copies ran while one was open for 0% of the time, Pallas kernels for 0%

profile of v4, /device:TPU:1, one launch (start us, length us, event | category | flops | bytes accessed | tf_op | source)
XLA Modules:
  0.0 108.5 jit_solution(10099982336535249627)
XLA Ops:
  0.0 1.5 %shard_map.55 = (f32[8,24,128]{2,1,0:T(8,128)}, f32[8,512]{1,0:T(8,128)}) custom-call(s32[1]{0:T(128)} %bitcast.core, s32[1]{0:T(128)} %bitcast.1.plane, s32[2,4]{1,0:T(2,128)} %domains.1, s32[2]{0:T(128)} %lengths.3, s32[64]{0:T(128)} %owner_map.1, f32[128,128]{1,0:T(8,128)} %bitcast.14), custom_call_target="tpu_custom_call" | custom-call | tf_op jit(solution)/shard_map/pallas_call | solution.py:107
  1.5 11.5 %all_to_all.15 = f32[8,24,128]{2,1,0:T(8,128)S(1)} all-to-all(f32[8,24,128]{2,1,0:T(8,128)} %get-tuple-element.9), channel_id=1, replica_groups=mesh['x'=4,'zh'=8,'zl'=2,'y'=4,'c'=2] {'zl','x'}, dimensions={0} | all-to-all | bytes 196608 | tf_op jit(solution)/shard_map/all_to_all | solution.py:116
  13.0 34.3 %all_gather.3.own = f32[64,16,128]{2,1,0:T(8,128)S(1)} all-gather(f32[8,16,128]{2,1,0:T(8,128)S(1)} %slice.25), channel_id=1, replica_groups={{0,17,32,49,64,81,96,113},{1,16,33,48,65,80,97,112},{2,19,34,51,66,83,9..., dimensions={0}, use_global_device_ids=true | all-gather | bytes 589824 | tf_op jit(solution)/shard_map/all_gather | solution.py:119
  47.3 2.8 %collective-permute-start = (f32[64,16,128]{2,1,0:T(8,128)S(1)}, f32[64,16,128]{2,1,0:T(8,128)S(1)}, u32[]{:S(2)}, u32[]{:S(2)}) collective-permute-start(f32[64,16,128]{2,1,0:T(8,128)S(1)} %all_gather.3.own), channel_id=1, source_target_pairs={{0,1},{1,0},{2,3},{3,2},{4,5},{5,4},{6,7},{7,6},{8,9},{9,8},{10,11... | collective-permute-start | bytes 1572872 | tf_op jit(solution)/shard_map/ppermute | solution.py:120
  50.2 0.1 convert_element_type.32.wanted
  50.3 1.4 %collective-permute-done.other = f32[64,16,128]{2,1,0:T(8,128)S(1)} collective-permute-done((f32[64,16,128]{2,1,0:T(8,128)S(1)}, f32[64,16,128]{2,1,0:T(8,128)S(1)}, u32[]{:S(2)}, u32[]{:S(2)}) %collective-permute-start) | collective-permute-done | bytes 524320 | tf_op jit(solution)/shard_map/ppermute | solution.py:120
  51.7 2.1 %shard_map.56 = f32[8,2,16,16,128]{4,3,2,1,0:T(8,128)} custom-call(s32[256]{0:T(256)S(1)} %convert_element_type.32.wanted, s32[1]{0:T(128)} %bitcast.core, s32[1]{0:T(128)} %bitcast.3.turn, f32[64,16,128]{2,1,0:T(8,128)S(1)} %all_gather.3.own, f32[64,16,128]{2,1,0:T(8,128)S(1)} %collective-permute-done.other), custom_call_target="tpu_custom_call" | custom-call | tf_op jit(solution)/shard_map/pallas_call | solution.py:121
  53.7 0.0 copy-start.1
  53.8 0.0 copy-start.2
  53.8 3.7 %all-to-all-start.1 = ((f32[8,2,16,16,128]{4,3,2,1,0:T(8,128)}), f32[8,2,16,16,128]{4,3,2,1,0:T(8,128)S(1)}, u32[]{:S(2)}, u32[]{:S(2)}) async-start(f32[8,2,16,16,128]{4,3,2,1,0:T(8,128)} %shard_map.56), calls=%async_computation.1 | async-start | bytes 4194304 | tf_op jit(solution)/shard_map/all_to_all | solution.py:130
  57.5 0.0 copy-start
  57.5 0.0 copy-done.1
  57.6 2.3 %collective-permute-start.1 = (f32[64,512]{1,0:T(8,128)S(1)}, f32[64,512]{1,0:T(8,128)S(1)}, u32[]{:S(2)}, u32[]{:S(2)}) collective-permute-start(f32[64,512]{1,0:T(8,128)S(1)} %get-tuple-element.21), channel_id=1, source_target_pairs={{0,1},{1,0},{2,3},{3,2},{4,5},{5,4},{6,7},{7,6},{8,9},{9,8},{10,11... | collective-permute-start | bytes 393224 | tf_op jit(solution)/shard_map/ppermute | solution.py:134
  59.9 0.0 copy-done.2
  59.9 0.9 collective-permute-done.1
  60.9 4.6 %collective-permute-start.4 = (f32[128,512]{1,0:T(8,128)S(1)}, f32[128,512]{1,0:T(8,128)S(1)}, u32[]{:S(2)}, u32[]{:S(2)}) collective-permute-start(f32[128,512]{1,0:T(8,128)S(1)} %get-tuple-element.14), channel_id=1, source_target_pairs={{0,6},{2,0},{4,2},{6,4},{1,7},{3,1},{5,3},{7,5},{8,14},{10,8},{12,... | collective-permute-start | bytes 786440 | tf_op jit(solution)/shard_map/ppermute | solution.py:138
  65.5 0.1 pad_add_fusion.places
  65.6 2.2 %collective-permute-start.3 = (f32[128,512]{1,0:T(8,128)S(1)}, f32[128,512]{1,0:T(8,128)S(1)}, u32[]{:S(2)}, u32[]{:S(2)}) collective-permute-start(f32[128,512]{1,0:T(8,128)S(1)} %get-tuple-element.14), channel_id=1, source_target_pairs={{0,4},{2,6},{4,0},{6,2},{1,5},{3,7},{5,1},{7,3},{8,12},{10,14},{12... | collective-permute-start | bytes 786440 | tf_op jit(solution)/shard_map/ppermute | solution.py:138
  67.9 2.6 %collective-permute-start.2 = (f32[128,512]{1,0:T(8,128)S(1)}, f32[128,512]{1,0:T(8,128)S(1)}, u32[]{:S(2)}, u32[]{:S(2)}) collective-permute-start(f32[128,512]{1,0:T(8,128)S(1)} %get-tuple-element.14), channel_id=1, source_target_pairs={{0,2},{2,4},{4,6},{6,0},{1,3},{3,5},{5,7},{7,1},{8,10},{10,12},{12... | collective-permute-start | bytes 786440 | tf_op jit(solution)/shard_map/ppermute | solution.py:138
  70.5 5.8 %collective-permute-done.4 = f32[128,512]{1,0:T(8,128)S(1)} collective-permute-done((f32[128,512]{1,0:T(8,128)S(1)}, f32[128,512]{1,0:T(8,128)S(1)}, u32[]{:S(2)}, u32[]{:S(2)}) %collective-permute-start.4) | collective-permute-done | bytes 262176 | tf_op jit(solution)/shard_map/ppermute | solution.py:138
  76.4 0.0 collective-permute-done.3
  76.4 6.4 %collective-permute-done.2 = f32[128,512]{1,0:T(8,128)S(1)} collective-permute-done((f32[128,512]{1,0:T(8,128)S(1)}, f32[128,512]{1,0:T(8,128)S(1)}, u32[]{:S(2)}, u32[]{:S(2)}) %collective-permute-start.2) | collective-permute-done | bytes 262176 | tf_op jit(solution)/shard_map/ppermute | solution.py:138
  82.9 0.8 all-to-all-done.1.tiles
  83.7 0.0 copy-done
  83.7 4.0 %shard_map.57 = f32[8,64,512]{2,1,0:T(8,128)S(1)} custom-call(s32[1]{0:T(128)} %bitcast.core, s32[4]{0:T(128)S(1)} %pad_add_fusion.places, s32[2]{0:T(128)S(1)} %copy-done, f32[8,2,16,16,128]{4,3,2,1,0:T(8,128)S(1)} %all-to-all-done.1.tiles, bf16[128,512]{1,0:T(8,128)(2,1)S(1)} %reduce-precision_convert_fusion.3.refs_0_, ...), custom_call_target="tpu_custom_call" | custom-call | tf_op jit(solution)/shard_map/pallas_call | solution.py:146
  87.7 20.0 %all_to_all.16 = f32[8,64,512]{2,1,0:T(8,128)S(1)} all-to-all(f32[8,64,512]{2,1,0:T(8,128)S(1)} %shard_map.57), channel_id=1, replica_groups=mesh['x'=4,'zh'=8,'zl'=2,'y'=4,'c'=2] {'c','y'}, dimensions={0} | all-to-all | bytes 2097152 | tf_op jit(solution)/shard_map/all_to_all | solution.py:159
  107.7 0.8 bitcast_reduce_fusion
  (9 shorter events, 0.3 us)
Async XLA Ops:
  47.3 4.4 %collective-permute-start = (f32[64,16,128]{2,1,0:T(8,128)S(1)}, f32[64,16,128]{2,1,0:T(8,128)S(1)}, u32[]{:S(2)}, u32[]{:S(2)}) collective-permute-start(f32[64,16,128]{2,1,0:T(8,128)S(1)} %all_gather.3.own), channel_id=1, source_target_pairs={{0,1},{1,0},{2,3},{3,2},{4,5},{5,4},{6,7},{7,6},{8,9},{9,8},{10,11... | collective-permute-start | bytes 1572872 | tf_op jit(solution)/shard_map/ppermute | solution.py:120
  53.7 3.8 %copy-start.1 = (f32[2,64,512]{2,1,0:T(8,128)S(1)}, f32[2,64,512]{2,1,0:T(8,128)}, u32[]{:S(2)}) copy-start(f32[2,64,512]{2,1,0:T(8,128)} %param.5) | copy-start | bytes 786436
  53.8 6.1 %copy-start.2 = (f32[8,512]{1,0:T(8,128)S(1)}, f32[8,512]{1,0:T(8,128)}, u32[]{:S(2)}) copy-start(f32[8,512]{1,0:T(8,128)} %get-tuple-element.12) | copy-start | bytes 49156
  53.8 29.9 %all-to-all-start.1 = ((f32[8,2,16,16,128]{4,3,2,1,0:T(8,128)}), f32[8,2,16,16,128]{4,3,2,1,0:T(8,128)S(1)}, u32[]{:S(2)}, u32[]{:S(2)}) async-start(f32[8,2,16,16,128]{4,3,2,1,0:T(8,128)} %shard_map.56), calls=%async_computation.1 | async-start | bytes 4194304 | tf_op jit(solution)/shard_map/all_to_all | solution.py:130
  57.5 26.1 %copy-start = (s32[2]{0:T(128)S(1)}, s32[2]{0:T(128)}, u32[]{:S(2)}) copy-start(s32[2]{0:T(128)} %lengths.3) | copy-start | bytes 28
  57.6 3.3 %collective-permute-start.1 = (f32[64,512]{1,0:T(8,128)S(1)}, f32[64,512]{1,0:T(8,128)S(1)}, u32[]{:S(2)}, u32[]{:S(2)}) collective-permute-start(f32[64,512]{1,0:T(8,128)S(1)} %get-tuple-element.21), channel_id=1, source_target_pairs={{0,1},{1,0},{2,3},{3,2},{4,5},{5,4},{6,7},{7,6},{8,9},{9,8},{10,11... | collective-permute-start | bytes 393224 | tf_op jit(solution)/shard_map/ppermute | solution.py:134
  60.9 15.4 %collective-permute-start.4 = (f32[128,512]{1,0:T(8,128)S(1)}, f32[128,512]{1,0:T(8,128)S(1)}, u32[]{:S(2)}, u32[]{:S(2)}) collective-permute-start(f32[128,512]{1,0:T(8,128)S(1)} %get-tuple-element.14), channel_id=1, source_target_pairs={{0,6},{2,0},{4,2},{6,4},{1,7},{3,1},{5,3},{7,5},{8,14},{10,8},{12,... | collective-permute-start | bytes 786440 | tf_op jit(solution)/shard_map/ppermute | solution.py:138
  65.6 10.8 %collective-permute-start.3 = (f32[128,512]{1,0:T(8,128)S(1)}, f32[128,512]{1,0:T(8,128)S(1)}, u32[]{:S(2)}, u32[]{:S(2)}) collective-permute-start(f32[128,512]{1,0:T(8,128)S(1)} %get-tuple-element.14), channel_id=1, source_target_pairs={{0,4},{2,6},{4,0},{6,2},{1,5},{3,7},{5,1},{7,3},{8,12},{10,14},{12... | collective-permute-start | bytes 786440 | tf_op jit(solution)/shard_map/ppermute | solution.py:138
  67.9 14.9 %collective-permute-start.2 = (f32[128,512]{1,0:T(8,128)S(1)}, f32[128,512]{1,0:T(8,128)S(1)}, u32[]{:S(2)}, u32[]{:S(2)}) collective-permute-start(f32[128,512]{1,0:T(8,128)S(1)} %get-tuple-element.14), channel_id=1, source_target_pairs={{0,2},{2,4},{4,6},{6,0},{1,3},{3,5},{5,7},{7,1},{8,10},{10,12},{12... | collective-permute-start | bytes 786440 | tf_op jit(solution)/shard_map/ppermute | solution.py:138

commit v5 on v4

--- a/solution.py
+++ b/solution.py
@@ -80,6 +80,8 @@
         rows = pl.ds(pl.multiple_of(places[i // 2] * TILE, TILE), TILE)
         (t_high, t_low)[i % 2][rows] = part[...]
     live = live_tiles(core, lengths)
+    rows = MT // (Y * C)
+    total = None
     for q in range(C):
         for a in range(M):
             for c in range(M):
@@ -88,9 +90,6 @@
                     at = a * TILE + g * SLICE
                     at = (q, slice(at, at + SLICE), slice(c * TILE, (c + 1) * TILE))
                     d_high[at], d_low[at] = split(tiles[g, q, a * M + c] * keep)
-    rows = MT // (Y * C)
-    total = None
-    for q in range(C):
         half = product((d_high[q], d_low[q]), (t_high[...], t_low[...]), ((1,), (0,)))
         term = product(split(half), (d_high[q], d_low[q]), ((1,), (1,)))
         total = term if total is None else total + term
@@ -107,11 +106,12 @@
     packed, mask = pl.pallas_call(
         pack_kernel,
         out_shape=[
-            jax.ShapeDtypeStruct((G, SLICE + 8, TILE), f32),
+            pltpu.VMEM((G, SLICE + 8, TILE), f32),
             jax.ShapeDtypeStruct((8, MT), f32),
         ],
         in_specs=[SMEM] * 5 + [VMEM],
         out_specs=[VMEM, VMEM],
+        compiler_params=pltpu.CompilerParams(vmem_limit_bytes=56 * 2**20),
     )(core, plane, domains, domain_length, owner_map, integral_store.reshape(TILE, TILE))
     spread = lax.all_to_all(packed, ("zl", "x"), split_axis=0, concat_axis=0, tiled=True)
     wanted = spread[:, SLICE, :pairs * KINDS].astype(jnp.int32).reshape(-1)

time: 109 us -> 109 us (level)
  no operation moved by 1% of the time
where the time goes in v5:
time: 109 us; the launch traced here: 108 us
  blocking collectives  65.6 us (60%)
  starting transfers between devices  18.4 us (17%)
  waiting for transfers between devices  15.3 us (14%)
  Pallas kernels  7.56 us (7%)
  other arithmetic  1.09 us (1%)
    all_gather x1, blocking collectives, on_device(): lax.all_gather(spread[:, :SLICE], ('zh', 'c'), axis=0, tiled=True, axis_i...  34.3 us
    all_to_all x1, blocking collectives, on_device(): lax.all_to_all(terms, ('c', 'y'), split_axis=0, concat_axis=0, tiled=True)  20 us
    ppermute x3, waiting for transfers between devices, on_device(): lax.ppermute(block, 'y', [(y, (y + step) % Y) for y in range(Y)])  12.2 us
    all_to_all x1, blocking collectives, on_device(): lax.all_to_all(packed, ('zl', 'x'), split_axis=0, concat_axis=0, tiled=True)  11.3 us
    ppermute x3, starting transfers between devices, on_device(): lax.ppermute(block, 'y', [(y, (y + step) % Y) for y in range(Y)])  9.49 us
    pallas_call x1, Pallas kernels, on_device(): pl.pallas_call(ladder_kernel, out_shape=jax.ShapeDtypeStruct((Y * C, rows...  4.03 us
    all_to_all x1, starting transfers between devices, on_device(): lax.all_to_all(picked, ('zl', 'x'), split_axis=0, concat_axis=0, tiled=True)  3.75 us
    ppermute x1, starting transfers between devices, on_device(): other = lax.ppermute(own, 'c', [(0, 1), (1, 0)])  2.85 us
  transfers between devices with their start and end apart: 6, of which 5 were waited for; matrix products, arithmetic and copies ran while one was open for 0% of the time, Pallas kernels for 0%

profile of v5, /device:TPU:1, one launch (start us, length us, event | category | flops | bytes accessed | tf_op | source)
XLA Modules:
  0.0 108.2 jit_solution(14163170707253772841)
XLA Ops:
  0.0 1.5 %shard_map.55 = (f32[8,24,128]{2,1,0:T(8,128)S(1)}, f32[8,512]{1,0:T(8,128)}) custom-call(s32[1]{0:T(128)} %bitcast.core, s32[1]{0:T(128)} %bitcast.1.plane, s32[2,4]{1,0:T(2,128)} %domains.1, s32[2]{0:T(128)} %lengths.3, s32[64]{0:T(128)} %owner_map.1, f32[128,128]{1,0:T(8,128)} %bitcast.14), custom_call_target="tpu_custom_call" | custom-call | tf_op jit(solution)/shard_map/pallas_call | solution.py:106
  1.5 11.3 %all_to_all.15 = f32[8,24,128]{2,1,0:T(8,128)S(1)} all-to-all(f32[8,24,128]{2,1,0:T(8,128)S(1)} %get-tuple-element.9), channel_id=1, replica_groups=mesh['x'=4,'zh'=8,'zl'=2,'y'=4,'c'=2] {'zl','x'}, dimensions={0} | all-to-all | bytes 196608 | tf_op jit(solution)/shard_map/all_to_all | solution.py:116
  12.8 34.3 %all_gather.3.own = f32[64,16,128]{2,1,0:T(8,128)S(1)} all-gather(f32[8,16,128]{2,1,0:T(8,128)S(1)} %slice.25), channel_id=1, replica_groups={{0,17,32,49,64,81,96,113},{1,16,33,48,65,80,97,112},{2,19,34,51,66,83,9..., dimensions={0}, use_global_device_ids=true | all-gather | bytes 589824 | tf_op jit(solution)/shard_map/all_gather | solution.py:119
  47.0 2.8 %collective-permute-start = (f32[64,16,128]{2,1,0:T(8,128)S(1)}, f32[64,16,128]{2,1,0:T(8,128)S(1)}, u32[]{:S(2)}, u32[]{:S(2)}) collective-permute-start(f32[64,16,128]{2,1,0:T(8,128)S(1)} %all_gather.3.own), channel_id=1, source_target_pairs={{0,1},{1,0},{2,3},{3,2},{4,5},{5,4},{6,7},{7,6},{8,9},{9,8},{10,11... | collective-permute-start | bytes 1572872 | tf_op jit(solution)/shard_map/ppermute | solution.py:120
  49.9 0.1 convert_element_type.32.wanted
  50.0 1.4 %collective-permute-done.other = f32[64,16,128]{2,1,0:T(8,128)S(1)} collective-permute-done((f32[64,16,128]{2,1,0:T(8,128)S(1)}, f32[64,16,128]{2,1,0:T(8,128)S(1)}, u32[]{:S(2)}, u32[]{:S(2)}) %collective-permute-start) | collective-permute-done | bytes 524320 | tf_op jit(solution)/shard_map/ppermute | solution.py:120
  51.4 2.1 %shard_map.56 = f32[8,2,16,16,128]{4,3,2,1,0:T(8,128)} custom-call(s32[256]{0:T(256)S(1)} %convert_element_type.32.wanted, s32[1]{0:T(128)} %bitcast.core, s32[1]{0:T(128)} %bitcast.3.turn, f32[64,16,128]{2,1,0:T(8,128)S(1)} %all_gather.3.own, f32[64,16,128]{2,1,0:T(8,128)S(1)} %collective-permute-done.other), custom_call_target="tpu_custom_call" | custom-call | tf_op jit(solution)/shard_map/pallas_call | solution.py:121
  53.5 0.0 copy-start.1
  53.5 0.0 copy-start.2
  53.5 3.7 %all-to-all-start.1 = ((f32[8,2,16,16,128]{4,3,2,1,0:T(8,128)}), f32[8,2,16,16,128]{4,3,2,1,0:T(8,128)S(1)}, u32[]{:S(2)}, u32[]{:S(2)}) async-start(f32[8,2,16,16,128]{4,3,2,1,0:T(8,128)} %shard_map.56), calls=%async_computation.1 | async-start | bytes 4194304 | tf_op jit(solution)/shard_map/all_to_all | solution.py:130
  57.2 0.0 copy-start
  57.3 0.0 copy-done.1
  57.3 2.3 %collective-permute-start.1 = (f32[64,512]{1,0:T(8,128)S(1)}, f32[64,512]{1,0:T(8,128)S(1)}, u32[]{:S(2)}, u32[]{:S(2)}) collective-permute-start(f32[64,512]{1,0:T(8,128)S(1)} %get-tuple-element.21), channel_id=1, source_target_pairs={{0,1},{1,0},{2,3},{3,2},{4,5},{5,4},{6,7},{7,6},{8,9},{9,8},{10,11... | collective-permute-start | bytes 393224 | tf_op jit(solution)/shard_map/ppermute | solution.py:134
  59.6 0.0 copy-done.2
  59.6 0.9 collective-permute-done.1
  60.6 4.6 %collective-permute-start.4 = (f32[128,512]{1,0:T(8,128)S(1)}, f32[128,512]{1,0:T(8,128)S(1)}, u32[]{:S(2)}, u32[]{:S(2)}) collective-permute-start(f32[128,512]{1,0:T(8,128)S(1)} %get-tuple-element.14), channel_id=1, source_target_pairs={{0,6},{2,0},{4,2},{6,4},{1,7},{3,1},{5,3},{7,5},{8,14},{10,8},{12,... | collective-permute-start | bytes 786440 | tf_op jit(solution)/shard_map/ppermute | solution.py:138
  65.3 0.1 pad_add_fusion.places
  65.4 2.2 %collective-permute-start.3 = (f32[128,512]{1,0:T(8,128)S(1)}, f32[128,512]{1,0:T(8,128)S(1)}, u32[]{:S(2)}, u32[]{:S(2)}) collective-permute-start(f32[128,512]{1,0:T(8,128)S(1)} %get-tuple-element.14), channel_id=1, source_target_pairs={{0,4},{2,6},{4,0},{6,2},{1,5},{3,7},{5,1},{7,3},{8,12},{10,14},{12... | collective-permute-start | bytes 786440 | tf_op jit(solution)/shard_map/ppermute | solution.py:138
  67.6 2.6 %collective-permute-start.2 = (f32[128,512]{1,0:T(8,128)S(1)}, f32[128,512]{1,0:T(8,128)S(1)}, u32[]{:S(2)}, u32[]{:S(2)}) collective-permute-start(f32[128,512]{1,0:T(8,128)S(1)} %get-tuple-element.14), channel_id=1, source_target_pairs={{0,2},{2,4},{4,6},{6,0},{1,3},{3,5},{5,7},{7,1},{8,10},{10,12},{12... | collective-permute-start | bytes 786440 | tf_op jit(solution)/shard_map/ppermute | solution.py:138
  70.3 5.8 %collective-permute-done.4 = f32[128,512]{1,0:T(8,128)S(1)} collective-permute-done((f32[128,512]{1,0:T(8,128)S(1)}, f32[128,512]{1,0:T(8,128)S(1)}, u32[]{:S(2)}, u32[]{:S(2)}) %collective-permute-start.4) | collective-permute-done | bytes 262176 | tf_op jit(solution)/shard_map/ppermute | solution.py:138
  76.1 0.0 collective-permute-done.3
  76.2 6.4 %collective-permute-done.2 = f32[128,512]{1,0:T(8,128)S(1)} collective-permute-done((f32[128,512]{1,0:T(8,128)S(1)}, f32[128,512]{1,0:T(8,128)S(1)}, u32[]{:S(2)}, u32[]{:S(2)}) %collective-permute-start.2) | collective-permute-done | bytes 262176 | tf_op jit(solution)/shard_map/ppermute | solution.py:138
  82.6 0.8 all-to-all-done.1.tiles
  83.4 0.0 copy-done
  83.4 4.0 %shard_map.57 = f32[8,64,512]{2,1,0:T(8,128)S(1)} custom-call(s32[1]{0:T(128)} %bitcast.core, s32[4]{0:T(128)S(1)} %pad_add_fusion.places, s32[2]{0:T(128)S(1)} %copy-done, f32[8,2,16,16,128]{4,3,2,1,0:T(8,128)S(1)} %all-to-all-done.1.tiles, bf16[128,512]{1,0:T(8,128)(2,1)S(1)} %reduce-precision_convert_fusion.3.refs_0_, ...), custom_call_target="tpu_custom_call" | custom-call | tf_op jit(solution)/shard_map/pallas_call | solution.py:146
  87.4 20.0 %all_to_all.16 = f32[8,64,512]{2,1,0:T(8,128)S(1)} all-to-all(f32[8,64,512]{2,1,0:T(8,128)S(1)} %shard_map.57), channel_id=1, replica_groups=mesh['x'=4,'zh'=8,'zl'=2,'y'=4,'c'=2] {'c','y'}, dimensions={0} | all-to-all | bytes 2097152 | tf_op jit(solution)/shard_map/all_to_all | solution.py:159
  107.4 0.8 bitcast_reduce_fusion
  (9 shorter events, 0.3 us)
Async XLA Ops:
  47.0 4.4 %collective-permute-start = (f32[64,16,128]{2,1,0:T(8,128)S(1)}, f32[64,16,128]{2,1,0:T(8,128)S(1)}, u32[]{:S(2)}, u32[]{:S(2)}) collective-permute-start(f32[64,16,128]{2,1,0:T(8,128)S(1)} %all_gather.3.own), channel_id=1, source_target_pairs={{0,1},{1,0},{2,3},{3,2},{4,5},{5,4},{6,7},{7,6},{8,9},{9,8},{10,11... | collective-permute-start | bytes 1572872 | tf_op jit(solution)/shard_map/ppermute | solution.py:120
  53.5 3.8 %copy-start.1 = (f32[2,64,512]{2,1,0:T(8,128)S(1)}, f32[2,64,512]{2,1,0:T(8,128)}, u32[]{:S(2)}) copy-start(f32[2,64,512]{2,1,0:T(8,128)} %param.5) | copy-start | bytes 786436
  53.5 6.1 %copy-start.2 = (f32[8,512]{1,0:T(8,128)S(1)}, f32[8,512]{1,0:T(8,128)}, u32[]{:S(2)}) copy-start(f32[8,512]{1,0:T(8,128)} %get-tuple-element.12) | copy-start | bytes 49156
  53.5 29.9 %all-to-all-start.1 = ((f32[8,2,16,16,128]{4,3,2,1,0:T(8,128)}), f32[8,2,16,16,128]{4,3,2,1,0:T(8,128)S(1)}, u32[]{:S(2)}, u32[]{:S(2)}) async-start(f32[8,2,16,16,128]{4,3,2,1,0:T(8,128)} %shard_map.56), calls=%async_computation.1 | async-start | bytes 4194304 | tf_op jit(solution)/shard_map/all_to_all | solution.py:130
  57.2 26.1 %copy-start = (s32[2]{0:T(128)S(1)}, s32[2]{0:T(128)}, u32[]{:S(2)}) copy-start(s32[2]{0:T(128)} %lengths.3) | copy-start | bytes 28
  57.3 3.3 %collective-permute-start.1 = (f32[64,512]{1,0:T(8,128)S(1)}, f32[64,512]{1,0:T(8,128)S(1)}, u32[]{:S(2)}, u32[]{:S(2)}) collective-permute-start(f32[64,512]{1,0:T(8,128)S(1)} %get-tuple-element.21), channel_id=1, source_target_pairs={{0,1},{1,0},{2,3},{3,2},{4,5},{5,4},{6,7},{7,6},{8,9},{9,8},{10,11... | collective-permute-start | bytes 393224 | tf_op jit(solution)/shard_map/ppermute | solution.py:134
  60.6 15.4 %collective-permute-start.4 = (f32[128,512]{1,0:T(8,128)S(1)}, f32[128,512]{1,0:T(8,128)S(1)}, u32[]{:S(2)}, u32[]{:S(2)}) collective-permute-start(f32[128,512]{1,0:T(8,128)S(1)} %get-tuple-element.14), channel_id=1, source_target_pairs={{0,6},{2,0},{4,2},{6,4},{1,7},{3,1},{5,3},{7,5},{8,14},{10,8},{12,... | collective-permute-start | bytes 786440 | tf_op jit(solution)/shard_map/ppermute | solution.py:138
  65.4 10.8 %collective-permute-start.3 = (f32[128,512]{1,0:T(8,128)S(1)}, f32[128,512]{1,0:T(8,128)S(1)}, u32[]{:S(2)}, u32[]{:S(2)}) collective-permute-start(f32[128,512]{1,0:T(8,128)S(1)} %get-tuple-element.14), channel_id=1, source_target_pairs={{0,4},{2,6},{4,0},{6,2},{1,5},{3,7},{5,1},{7,3},{8,12},{10,14},{12... | collective-permute-start | bytes 786440 | tf_op jit(solution)/shard_map/ppermute | solution.py:138
  67.6 14.9 %collective-permute-start.2 = (f32[128,512]{1,0:T(8,128)S(1)}, f32[128,512]{1,0:T(8,128)S(1)}, u32[]{:S(2)}, u32[]{:S(2)}) collective-permute-start(f32[128,512]{1,0:T(8,128)S(1)} %get-tuple-element.14), channel_id=1, source_target_pairs={{0,2},{2,4},{4,6},{6,0},{1,3},{3,5},{5,7},{7,1},{8,10},{10,12},{12... | collective-permute-start | bytes 786440 | tf_op jit(solution)/shard_map/ppermute | solution.py:138

commit v6 on v5

--- a/solution.py
+++ b/solution.py
@@ -1,3 +1,5 @@
+import functools
+
 import jax
 import jax.numpy as jnp
 from jax import lax
@@ -41,17 +43,14 @@
     mask[...] = jnp.where((tile < length) & (column < length * TILE), 1.0, 0.0).astype(f32)
 
 
-def pick_kernel(wanted, core, turn, own, other, out, held, sems):
+def pick_kernel(vector, wanted, core, gathered, *refs):
+    out, held, sems = refs[-3:]
     first = core[0] * KINDS
     copies = []
     for g in range(G):
         for k in range(KINDS):
-            row = wanted[g * C * KINDS + first + k]
-            mine = lax.rem(lax.div(row, G), 2) == turn[0]
-            a, b = own[row], other[row]
-            held[g, 0, k] = jnp.where(mine, a, b)
-            held[g, 1, k] = jnp.where(mine, b, a)
-        copies.append(pltpu.make_async_copy(held.at[g], out.at[g], sems.at[g]))
+            held[g, k] = gathered[wanted[g * C * KINDS + first + k]]
+        copies.append(pltpu.make_async_copy(held.at[g], out.at[g, vector], sems.at[g]))
         copies[-1].start()
     for copy in copies:
         copy.wait()
@@ -74,7 +73,7 @@
     return [jnp.where(a < length, 1.0, 0.0).astype(f32) for a in range(M)]
 
 
-def ladder_kernel(core, places, lengths, tiles, *refs):
+def ladder_kernel(core, turn, places, domains, owner_map, lengths, tiles, *refs):
     parts, (out, d_high, d_low, t_high, t_low) = refs[:2 * Y], refs[2 * Y:]
     for i, part in enumerate(parts):
         rows = pl.ds(pl.multiple_of(places[i // 2] * TILE, TILE), TILE)
@@ -86,10 +85,12 @@
         for a in range(M):
             for c in range(M):
                 keep = live[a] * live[c]
+                place = owner_map[domains[core[0], a] * NT + domains[core[0], c]]
+                vector = lax.rem(q + turn[0] + lax.div(lax.rem(place, ZH * ZL), ZL), C)
                 for g in range(G):
                     at = a * TILE + g * SLICE
                     at = (q, slice(at, at + SLICE), slice(c * TILE, (c + 1) * TILE))
-                    d_high[at], d_low[at] = split(tiles[g, q, a * M + c] * keep)
+                    d_high[at], d_low[at] = split(tiles[g, vector, a * M + c] * keep)
         half = product((d_high[q], d_low[q]), (t_high[...], t_low[...]), ((1,), (0,)))
         term = product(split(half), (d_high[q], d_low[q]), ((1,), (1,)))
         total = term if total is None else total + term
@@ -118,14 +119,19 @@
     groups = [[C * z + (z + g) % C for z in range(ZH)] for g in range(C)]
     own = lax.all_gather(spread[:, :SLICE], ("zh", "c"), axis=0, tiled=True, axis_index_groups=groups)
     other = lax.ppermute(own, "c", [(0, 1), (1, 0)])
-    picked = pl.pallas_call(
-        pick_kernel,
-        out_shape=pltpu.HBM((G, C, KINDS, SLICE, TILE), f32),
-        in_specs=[SMEM, SMEM, SMEM, VMEM, VMEM],
-        out_specs=pl.BlockSpec(memory_space=pltpu.HBM),
-        scratch_shapes=[pltpu.VMEM((G, C, KINDS, SLICE, TILE), f32), pltpu.SemaphoreType.DMA((G,))],
-        compiler_params=SMALL,
-    )(wanted, core, turn, own, other)
+    def pick(vector, gathered, *filled):
+        hbm = pl.BlockSpec(memory_space=pltpu.HBM)
+        return pl.pallas_call(
+            functools.partial(pick_kernel, vector),
+            out_shape=pltpu.HBM((G, C, KINDS, SLICE, TILE), f32),
+            in_specs=[SMEM, SMEM, VMEM] + [hbm] * len(filled),
+            out_specs=hbm,
+            scratch_shapes=[pltpu.VMEM((G, KINDS, SLICE, TILE), f32), pltpu.SemaphoreType.DMA((G,))],
+            input_output_aliases={3: 0} if filled else {},
+            compiler_params=SMALL,
+        )(wanted, core, gathered, *filled)
+
+    picked = pick(1, other, pick(0, own))
     picked, amplitudes = lax.optimization_barrier((picked, amplitudes))
     tiles = lax.all_to_all(picked, ("zl", "x"), split_axis=0, concat_axis=0, tiled=True)
 
@@ -146,7 +152,7 @@
     terms = pl.pallas_call(
         ladder_kernel,
         out_shape=jax.ShapeDtypeStruct((Y * C, rows, MT), f32),
-        in_specs=[SMEM, SMEM, SMEM, VMEM] + [VMEM] * (2 * Y),
+        in_specs=[SMEM] * 6 + [VMEM] * (1 + 2 * Y),
         out_specs=VMEM,
         scratch_shapes=[
             pltpu.VMEM((C, MT, MT), bf16),
@@ -155,7 +161,7 @@
             pltpu.VMEM((MT, MT), bf16),
         ],
         compiler_params=pltpu.CompilerParams(vmem_limit_bytes=24 * 2**20),
-    )(core, places, domain_length, tiles, *masked)
+    )(core, turn, places, domains, owner_map, domain_length, tiles, *masked)
     parts = lax.all_to_all(terms, ("c", "y"), split_axis=0, concat_axis=0, tiled=True)
     return parts.reshape(pairs, Y, rows, MT).sum(1)
 

time: 109 us -> 109 us (level)
  Pallas kernels: 7.56 us -> 8.79 us
  waiting for transfers between devices: 15.3 us -> 14.1 us
    ppermute x1, waiting for transfers between devices: 1.41 us -> 0.01 us  [on_device(): other = lax.ppermute(own, 'c', [(0, 1), (1, 0)])]
    pallas_call x1 -> x2, Pallas kernels: 2.06 us -> 3.25 us  [pick(): pl.pallas_call(functools.partial(pick_kernel, vector), out_shape=pltpu.HB...]
  transfers between devices with their start and end apart: 6 -> 6, of which waited for: 5 -> 4; matrix products, arithmetic and copies ran while one was open for 0% -> 0% of each run, Pallas kernels for 0% -> 1%
where the time goes in v6:
time: 109 us; the launch traced here: 108 us
  blocking collectives  65.5 us (60%)
  starting transfers between devices  18.2 us (17%)
  waiting for transfers between devices  14.1 us (13%)
  Pallas kernels  8.79 us (8%)
  other arithmetic  1.09 us (1%)
    all_gather x1, blocking collectives, on_device(): lax.all_gather(spread[:, :SLICE], ('zh', 'c'), axis=0, tiled=True, axis_i...  34.3 us
    all_to_all x1, blocking collectives, on_device(): lax.all_to_all(terms, ('c', 'y'), split_axis=0, concat_axis=0, tiled=True)  20 us
    ppermute x3, waiting for transfers between devices, on_device(): lax.ppermute(block, 'y', [(y, (y + step) % Y) for y in range(Y)])  12.2 us
    all_to_all x1, blocking collectives, on_device(): lax.all_to_all(packed, ('zl', 'x'), split_axis=0, concat_axis=0, tiled=True)  11.3 us
    ppermute x3, starting transfers between devices, on_device(): lax.ppermute(block, 'y', [(y, (y + step) % Y) for y in range(Y)])  9.49 us
    pallas_call x1, Pallas kernels, on_device(): pl.pallas_call(ladder_kernel, out_shape=jax.ShapeDtypeStruct((Y * C, rows...  4.07 us
    all_to_all x1, starting transfers between devices, on_device(): lax.all_to_all(picked, ('zl', 'x'), split_axis=0, concat_axis=0, tiled=True)  3.75 us
    pallas_call x2, Pallas kernels, pick(): pl.pallas_call(functools.partial(pick_kernel, vector), out_shape=pltpu.HB...  3.25 us
  transfers between devices with their start and end apart: 6, of which 4 were waited for; matrix products, arithmetic and copies ran while one was open for 0% of the time, Pallas kernels for 1%

profile of v6, /device:TPU:1, one launch (start us, length us, event | category | flops | bytes accessed | tf_op | source)
XLA Modules:
  0.0 108.1 jit_solution(10025148469037226109)
XLA Ops:
  0.0 1.5 %shard_map.55 = (f32[8,24,128]{2,1,0:T(8,128)S(1)}, f32[8,512]{1,0:T(8,128)}) custom-call(s32[1]{0:T(128)} %bitcast.core, s32[1]{0:T(128)} %bitcast.2.plane, s32[2,4]{1,0:T(2,128)} %domains.3, s32[2]{0:T(128)} %lengths.3, s32[64]{0:T(128)} %owner_map.3, f32[128,128]{1,0:T(8,128)} %bitcast.14), custom_call_target="tpu_custom_call" | custom-call | tf_op jit(solution)/shard_map/pallas_call | solution.py:107
  1.5 11.3 %all_to_all.15 = f32[8,24,128]{2,1,0:T(8,128)S(1)} all-to-all(f32[8,24,128]{2,1,0:T(8,128)S(1)} %get-tuple-element.9), channel_id=1, replica_groups=mesh['x'=4,'zh'=8,'zl'=2,'y'=4,'c'=2] {'zl','x'}, dimensions={0} | all-to-all | bytes 196608 | tf_op jit(solution)/shard_map/all_to_all | solution.py:117
  12.8 34.3 %all_gather.3.gathered = f32[64,16,128]{2,1,0:T(8,128)S(1)} all-gather(f32[8,16,128]{2,1,0:T(8,128)S(1)} %slice.25), channel_id=1, replica_groups={{0,17,32,49,64,81,96,113},{1,16,33,48,65,80,97,112},{2,19,34,51,66,83,9..., dimensions={0}, use_global_device_ids=true | all-gather | bytes 589824 | tf_op jit(solution)/shard_map/all_gather | solution.py:120
  47.0 2.8 %collective-permute-start = (f32[64,16,128]{2,1,0:T(8,128)S(1)}, f32[64,16,128]{2,1,0:T(8,128)S(1)}, u32[]{:S(2)}, u32[]{:S(2)}) collective-permute-start(f32[64,16,128]{2,1,0:T(8,128)S(1)} %all_gather.3.gathered), channel_id=1, source_target_pairs={{0,1},{1,0},{2,3},{3,2},{4,5},{5,4},{6,7},{7,6},{8,9},{9,8},{10,11... | collective-permute-start | bytes 1572872 | tf_op jit(solution)/shard_map/ppermute | solution.py:121
  49.9 0.1 convert_element_type.32.wanted
  50.0 1.6 %shard_map.56.refs_0_ = f32[8,2,16,16,128]{4,3,2,1,0:T(8,128)} custom-call(s32[256]{0:T(256)S(1)} %convert_element_type.32.wanted, s32[1]{0:T(128)} %bitcast.core, f32[64,16,128]{2,1,0:T(8,128)S(1)} %all_gather.3.gathered), custom_call_target="tpu_custom_call" | custom-call | tf_op jit(solution)/shard_map/pallas_call | solution.py:124
  51.6 0.0 collective-permute-done.gathered
  51.6 1.7 %shard_map.57 = f32[8,2,16,16,128]{4,3,2,1,0:T(8,128)} custom-call(s32[256]{0:T(256)S(1)} %convert_element_type.32.wanted, s32[1]{0:T(128)} %bitcast.core, f32[64,16,128]{2,1,0:T(8,128)S(1)} %collective-permute-done.gathered, f32[8,2,16,16,128]{4,3,2,1,0:T(8,128)} %shard_map.56.refs_0_), custom_call_target="tpu_custom_call", output_to_operand_aliasing={{}: (3, {})} | custom-call | tf_op jit(solution)/shard_map/pallas_call | solution.py:124
  53.3 0.0 copy-start.3
  53.3 0.0 copy-start.4
  53.3 3.7 %all-to-all-start.1 = ((f32[8,2,16,16,128]{4,3,2,1,0:T(8,128)}), f32[8,2,16,16,128]{4,3,2,1,0:T(8,128)S(1)}, u32[]{:S(2)}, u32[]{:S(2)}) async-start(f32[8,2,16,16,128]{4,3,2,1,0:T(8,128)} %shard_map.57), calls=%async_computation.1 | async-start | bytes 4194304 | tf_op jit(solution)/shard_map/all_to_all | solution.py:136
  57.0 0.0 copy-start
  57.1 0.0 copy-start.1
  57.1 0.0 copy-start.2
  57.1 0.0 copy-done.3
  57.1 2.1 %collective-permute-start.1 = (f32[64,512]{1,0:T(8,128)S(1)}, f32[64,512]{1,0:T(8,128)S(1)}, u32[]{:S(2)}, u32[]{:S(2)}) collective-permute-start(f32[64,512]{1,0:T(8,128)S(1)} %get-tuple-element.21), channel_id=1, source_target_pairs={{0,1},{1,0},{2,3},{3,2},{4,5},{5,4},{6,7},{7,6},{8,9},{9,8},{10,11... | collective-permute-start | bytes 393224 | tf_op jit(solution)/shard_map/ppermute | solution.py:140
  59.2 0.0 copy-done.4
  59.3 1.1 %collective-permute-done.1 = f32[64,512]{1,0:T(8,128)S(1)} collective-permute-done((f32[64,512]{1,0:T(8,128)S(1)}, f32[64,512]{1,0:T(8,128)S(1)}, u32[]{:S(2)}, u32[]{:S(2)}) %collective-permute-start.1) | collective-permute-done | bytes 131104 | tf_op jit(solution)/shard_map/ppermute | solution.py:140
  60.4 4.6 %collective-permute-start.4 = (f32[128,512]{1,0:T(8,128)S(1)}, f32[128,512]{1,0:T(8,128)S(1)}, u32[]{:S(2)}, u32[]{:S(2)}) collective-permute-start(f32[128,512]{1,0:T(8,128)S(1)} %get-tuple-element.14), channel_id=1, source_target_pairs={{0,6},{2,0},{4,2},{6,4},{1,7},{3,1},{5,3},{7,5},{8,14},{10,8},{12,... | collective-permute-start | bytes 786440 | tf_op jit(solution)/shard_map/ppermute | solution.py:144
  65.1 0.1 pad_add_fusion.places
  65.2 2.2 %collective-permute-start.3 = (f32[128,512]{1,0:T(8,128)S(1)}, f32[128,512]{1,0:T(8,128)S(1)}, u32[]{:S(2)}, u32[]{:S(2)}) collective-permute-start(f32[128,512]{1,0:T(8,128)S(1)} %get-tuple-element.14), channel_id=1, source_target_pairs={{0,4},{2,6},{4,0},{6,2},{1,5},{3,7},{5,1},{7,3},{8,12},{10,14},{12... | collective-permute-start | bytes 786440 | tf_op jit(solution)/shard_map/ppermute | solution.py:144
  67.5 2.6 %collective-permute-start.2 = (f32[128,512]{1,0:T(8,128)S(1)}, f32[128,512]{1,0:T(8,128)S(1)}, u32[]{:S(2)}, u32[]{:S(2)}) collective-permute-start(f32[128,512]{1,0:T(8,128)S(1)} %get-tuple-element.14), channel_id=1, source_target_pairs={{0,2},{2,4},{4,6},{6,0},{1,3},{3,5},{5,7},{7,1},{8,10},{10,12},{12... | collective-permute-start | bytes 786440 | tf_op jit(solution)/shard_map/ppermute | solution.py:144
  70.1 6.0 %collective-permute-done.4 = f32[128,512]{1,0:T(8,128)S(1)} collective-permute-done((f32[128,512]{1,0:T(8,128)S(1)}, f32[128,512]{1,0:T(8,128)S(1)}, u32[]{:S(2)}, u32[]{:S(2)}) %collective-permute-start.4) | collective-permute-done | bytes 262176 | tf_op jit(solution)/shard_map/ppermute | solution.py:144
  76.1 0.0 collective-permute-done.3
  76.2 6.2 %collective-permute-done.2 = f32[128,512]{1,0:T(8,128)S(1)} collective-permute-done((f32[128,512]{1,0:T(8,128)S(1)}, f32[128,512]{1,0:T(8,128)S(1)}, u32[]{:S(2)}, u32[]{:S(2)}) %collective-permute-start.2) | collective-permute-done | bytes 262176 | tf_op jit(solution)/shard_map/ppermute | solution.py:144
  82.4 0.8 all-to-all-done.1.tiles
  83.2 0.0 copy-done
  83.2 0.0 copy-done.1
  83.2 0.0 copy-done.2
  83.2 4.1 %shard_map.58 = f32[8,64,512]{2,1,0:T(8,128)S(1)} custom-call(s32[1]{0:T(128)} %bitcast.core, s32[1]{0:T(128)} %bitcast.1.turn, s32[4]{0:T(128)S(1)} %pad_add_fusion.places, s32[2,4]{1,0:T(2,128)S(1)} %copy-done, s32[64]{0:T(128)S(1)} %copy-done.1, s32[2]{0:T(128)S(1)} %copy-done.2, f32[8,2,16,16,128]{4,3,2,1,0:T(8,128)S(1)} %all-to-all-done.1.tiles, ...), custom_call_target="tpu_custom_call" | custom-call | tf_op jit(solution)/shard_map/pallas_call | solution.py:152
  87.3 20.0 %all_to_all.16 = f32[8,64,512]{2,1,0:T(8,128)S(1)} all-to-all(f32[8,64,512]{2,1,0:T(8,128)S(1)} %shard_map.58), channel_id=1, replica_groups=mesh['x'=4,'zh'=8,'zl'=2,'y'=4,'c'=2] {'c','y'}, dimensions={0} | all-to-all | bytes 2097152 | tf_op jit(solution)/shard_map/all_to_all | solution.py:165
  107.3 0.8 bitcast_reduce_fusion
  (9 shorter events, 0.3 us)
Async XLA Ops:
  47.0 4.6 %collective-permute-start = (f32[64,16,128]{2,1,0:T(8,128)S(1)}, f32[64,16,128]{2,1,0:T(8,128)S(1)}, u32[]{:S(2)}, u32[]{:S(2)}) collective-permute-start(f32[64,16,128]{2,1,0:T(8,128)S(1)} %all_gather.3.gathered), channel_id=1, source_target_pairs={{0,1},{1,0},{2,3},{3,2},{4,5},{5,4},{6,7},{7,6},{8,9},{9,8},{10,11... | collective-permute-start | bytes 1572872 | tf_op jit(solution)/shard_map/ppermute | solution.py:121
  53.3 3.8 %copy-start.3 = (f32[2,64,512]{2,1,0:T(8,128)S(1)}, f32[2,64,512]{2,1,0:T(8,128)}, u32[]{:S(2)}) copy-start(f32[2,64,512]{2,1,0:T(8,128)} %param.5) | copy-start | bytes 786436
  53.3 6.0 %copy-start.4 = (f32[8,512]{1,0:T(8,128)S(1)}, f32[8,512]{1,0:T(8,128)}, u32[]{:S(2)}) copy-start(f32[8,512]{1,0:T(8,128)} %get-tuple-element.12) | copy-start | bytes 49156
  53.3 29.9 %all-to-all-start.1 = ((f32[8,2,16,16,128]{4,3,2,1,0:T(8,128)}), f32[8,2,16,16,128]{4,3,2,1,0:T(8,128)S(1)}, u32[]{:S(2)}, u32[]{:S(2)}) async-start(f32[8,2,16,16,128]{4,3,2,1,0:T(8,128)} %shard_map.57), calls=%async_computation.1 | async-start | bytes 4194304 | tf_op jit(solution)/shard_map/all_to_all | solution.py:136
  57.0 26.2 %copy-start = (s32[2,4]{1,0:T(2,128)S(1)}, s32[2,4]{1,0:T(2,128)}, u32[]{:S(2)}) copy-start(s32[2,4]{1,0:T(2,128)} %domains.3) | copy-start | bytes 100
  57.1 26.2 %copy-start.1 = (s32[64]{0:T(128)S(1)}, s32[64]{0:T(128)}, u32[]{:S(2)}) copy-start(s32[64]{0:T(128)} %owner_map.3) | copy-start | bytes 772
  57.1 26.2 %copy-start.2 = (s32[2]{0:T(128)S(1)}, s32[2]{0:T(128)}, u32[]{:S(2)}) copy-start(s32[2]{0:T(128)} %lengths.3) | copy-start | bytes 28
  57.1 3.2 %collective-permute-start.1 = (f32[64,512]{1,0:T(8,128)S(1)}, f32[64,512]{1,0:T(8,128)S(1)}, u32[]{:S(2)}, u32[]{:S(2)}) collective-permute-start(f32[64,512]{1,0:T(8,128)S(1)} %get-tuple-element.21), channel_id=1, source_target_pairs={{0,1},{1,0},{2,3},{3,2},{4,5},{5,4},{6,7},{7,6},{8,9},{9,8},{10,11... | collective-permute-start | bytes 393224 | tf_op jit(solution)/shard_map/ppermute | solution.py:140
  60.4 15.6 %collective-permute-start.4 = (f32[128,512]{1,0:T(8,128)S(1)}, f32[128,512]{1,0:T(8,128)S(1)}, u32[]{:S(2)}, u32[]{:S(2)}) collective-permute-start(f32[128,512]{1,0:T(8,128)S(1)} %get-tuple-element.14), channel_id=1, source_target_pairs={{0,6},{2,0},{4,2},{6,4},{1,7},{3,1},{5,3},{7,5},{8,14},{10,8},{12,... | collective-permute-start | bytes 786440 | tf_op jit(solution)/shard_map/ppermute | solution.py:144
  65.2 11.0 %collective-permute-start.3 = (f32[128,512]{1,0:T(8,128)S(1)}, f32[128,512]{1,0:T(8,128)S(1)}, u32[]{:S(2)}, u32[]{:S(2)}) collective-permute-start(f32[128,512]{1,0:T(8,128)S(1)} %get-tuple-element.14), channel_id=1, source_target_pairs={{0,4},{2,6},{4,0},{6,2},{1,5},{3,7},{5,1},{7,3},{8,12},{10,14},{12... | collective-permute-start | bytes 786440 | tf_op jit(solution)/shard_map/ppermute | solution.py:144
  67.5 14.9 %collective-permute-start.2 = (f32[128,512]{1,0:T(8,128)S(1)}, f32[128,512]{1,0:T(8,128)S(1)}, u32[]{:S(2)}, u32[]{:S(2)}) collective-permute-start(f32[128,512]{1,0:T(8,128)S(1)} %get-tuple-element.14), channel_id=1, source_target_pairs={{0,2},{2,4},{4,6},{6,0},{1,3},{3,5},{5,7},{7,1},{8,10},{10,12},{12... | collective-permute-start | bytes 786440 | tf_op jit(solution)/shard_map/ppermute | solution.py:144
